TPU v7x, 512 devices: a whole 4x4x16 slice. The times are simulated.
512 devices in a mesh: seq: 64 (over z_hi, x, y, core), head: 8 (over z_lo).
Axes of the slice: x: 4, y: 4, z: 16 (z_hi: 2, z_lo: 8; z = z_hi * 8 + z_lo), core: 2. Of those that a mesh axis runs over, the one named last changes fastest.
Arguments:
- queries: bfloat16 [32768, 12288], P('seq', 'head'), may hold values from -100 to 100
- latent: bfloat16 [32768, 512], P('seq', 'head'), may hold values from -6 to 6
- key_rope: bfloat16 [32768, 64], P('seq'), may hold values from -6 to 6
- key_up: bfloat16 [512, 8192], P(None, 'head'), may hold values from -0.25 to 0.25
- value_up: bfloat16 [512, 8192], P(None, 'head'), may hold values from -0.25 to 0.25
- block_ids: int32 [128], P('seq'), may hold values from 0 to 127, each once
Outputs:
- attended: bfloat16 [32768, 8192], P('seq', 'head')
Inputs may be any that keep to these rules, and one draw needn't show every extreme that they name: `block_ids`: every block number appears once.
All inputs are finite; a program needn't handle non-finite values.
Results may differ from a plain program's by a relative error of at most 0.006.
Values may be sent and summed in bfloat16 or wider, within the bound.
No kernel may reach another device: no remote copies, remote signals or barrier semaphores. Data moves between devices by JAX's collectives and lax.ppermute only.
A program may use at most 64 MiB of HBM per device.

v0:
```python
import jax
import jax.numpy as jnp
from jax import lax
from jax.sharding import PartitionSpec as P

ROPE = 64
NOPE = 128
VAL = 128


def shifted(shard, axis, by):
    peers = lax.axis_size(axis)
    return lax.ppermute(shard, axis, [(i, (i + by) % peers) for i in range(peers)])


def project_rows(latent_full, key_up, value_up):
    key_part = jnp.dot(latent_full, key_up, preferred_element_type=jnp.float32).astype(jnp.bfloat16)
    value_part = jnp.dot(latent_full, value_up, preferred_element_type=jnp.float32).astype(
        jnp.bfloat16
    )
    return (key_part, value_part)


def positions_of(ids_pair, row_count):
    half_rows = row_count // 2
    row_ids = jnp.arange(row_count, dtype=jnp.int32)
    return ids_pair[row_ids // half_rows] * half_rows + row_ids % half_rows


def shards(queries, latent, key_rope, key_up, value_up, block_ids):
    row_count = queries.shape[0]
    head_count = key_up.shape[1] // NOPE
    latent_full = lax.all_gather(latent, "head", axis=1, tiled=True)
    prior_latent, prior_rope, prior_ids = shifted((latent_full, key_rope, block_ids), "seq", 1)
    both_latent = jnp.concatenate([latent_full, prior_latent], axis=0)
    key_all, value_all = project_rows(both_latent, key_up, value_up)
    rope_all = jnp.concatenate([key_rope, prior_rope], axis=0)
    query_pos = positions_of(block_ids, row_count)
    key_pos = jnp.concatenate([query_pos, positions_of(prior_ids, row_count)], axis=0)
    allowed = key_pos[None, :] <= query_pos[:, None]
    score_scale = 1.0 / jnp.sqrt(jnp.float32(NOPE + ROPE))
    width = NOPE + ROPE
    results = []
    for head in range(head_count):
        query_nope = queries[:, head * width : head * width + NOPE]
        query_rope = queries[:, head * width + NOPE : (head + 1) * width]
        key_head = key_all[:, head * NOPE : (head + 1) * NOPE]
        value_head = value_all[:, head * VAL : (head + 1) * VAL]
        score = jnp.einsum("qd,kd->qk", query_nope, key_head, preferred_element_type=jnp.float32)
        score = score + jnp.einsum(
            "qd,kd->qk", query_rope, rope_all, preferred_element_type=jnp.float32
        )
        score = score * score_scale
        score = jnp.where(allowed, score, jnp.float32(-1e30))
        top = jnp.max(score, axis=-1, keepdims=True)
        weight = jnp.where(allowed, jnp.exp(score - top), jnp.float32(0.0))
        total = jnp.sum(weight, axis=-1, keepdims=True)
        summed = jnp.dot(
            weight.astype(jnp.bfloat16), value_head, preferred_element_type=jnp.float32
        )
        results.append((summed / total).astype(jnp.bfloat16))
    return jnp.concatenate(results, axis=1)


def solution(mesh):
    in_specs = (
        P("seq", "head"),
        P("seq", "head"),
        P("seq", None),
        P(None, "head"),
        P(None, "head"),
        P("seq"),
    )
    out_specs = P("seq", "head")
    return jax.shard_map(shards, mesh=mesh, in_specs=in_specs, out_specs=out_specs, check_vma=False)
```

profile of v0, /device:TPU:0, one launch (start us, length us, event | category | flops | bytes accessed | tf_op | source)
XLA Modules:
  0.0 111.2 jit_solution(7430149171717792585)
XLA Ops:
  0.0 2.0 %collective-permute-start = (s32[2]{0:T(128)}, s32[2]{0:T(128)S(1)}, u32[]{:S(2)}, u32[]{:S(2)}) collective-permute-start(s32[2]{0:T(128)} %param.11), channel_id=1, source_target_pairs={{0,8},{8,16},{16,24},{24,32},{32,40},{40,48},{48,56},{56,64},{64,7... | collective-permute-start | bytes 32 | tf_op jit(solution)/shard_map/ppermute | solution.py:13
  2.1 48.1 %all_gather.3 = bf16[512,512]{0,1:T(8,128)(2,1)S(1)} all-gather(bf16[512,64]{0,1:T(8,128)(2,1)} %param.7), channel_id=1, replica_groups=mesh['seq'=64,'head'=8] {'head'}, dimensions={1}, use_global_device_ids=true | all-gather | bytes 589824 | tf_op jit(solution)/shard_map/all_gather | solution.py:33
  50.2 1.9 %collective-permute-start.1 = (bf16[512,512]{0,1:T(8,128)(2,1)S(1)}, bf16[512,512]{0,1:T(8,128)(2,1)S(1)}, u32[]{:S(2)}, u32[]{:S(2)}) collective-permute-start(bf16[512,512]{0,1:T(8,128)(2,1)S(1)} %all_gather.3), channel_id=1, source_target_pairs={{0,8},{8,16},{16,24},{24,32},{32,40},{40,48},{48,56},{56,64},{64,7... | collective-permute-start | bytes 1572872 | tf_op jit(solution)/shard_map/ppermute | solution.py:13
  52.1 1.9 %collective-permute-start.2 = (bf16[512,64]{0,1:T(8,128)(2,1)}, bf16[512,64]{0,1:T(8,128)(2,1)S(1)}, u32[]{:S(2)}, u32[]{:S(2)}) collective-permute-start(bf16[512,64]{0,1:T(8,128)(2,1)} %param.8), channel_id=1, source_target_pairs={{0,8},{8,16},{16,24},{24,32},{32,40},{40,48},{48,56},{56,64},{64,7... | collective-permute-start | bytes 196616 | tf_op jit(solution)/shard_map/ppermute | solution.py:13
  54.0 1.3 %fusion.136 = (s32[1]{0:T(128)}, s32[1]{0:T(128)}) fusion(s32[2]{0:T(128)} %param.11), kind=kLoop, calls=%fused_computation.136 | loop fusion | bytes 16 | tf_op jit(solution)/shard_map/gather | solution.py:27
  55.4 0.9 constant_dynamic-update-slice_fusion.3
  56.3 1.3 %fusion.89 = s32[512,1]{0,1:T(1,128)S(1)} fusion(s32[]{:T(128)} %bitcast.1, s32[]{:T(128)} %bitcast), kind=kLoop, calls=%fused_computation.120 | loop fusion | flops 7168 | bytes 2056 | tf_op jit(solution)/shard_map/mul | solution.py:27
  57.6 0.6 fusion.135
  58.2 1.3 %fusion.88 = s32[512,1]{0,1:T(1,128)S(1)} fusion(s32[]{:T(128)} %bitcast.4, s32[]{:T(128)} %bitcast.3), kind=kLoop, calls=%fused_computation.119 | loop fusion | flops 7168 | bytes 2056 | tf_op jit(solution)/shard_map/mul | solution.py:27
  59.6 29.5 %collective-permute-done.2 = bf16[512,64]{0,1:T(8,128)(2,1)S(1)} collective-permute-done((bf16[512,64]{0,1:T(8,128)(2,1)}, bf16[512,64]{0,1:T(8,128)(2,1)S(1)}, u32[]{:S(2)}, u32[]{:S(2)}) %collective-permute-start.2) | collective-permute-done | bytes 65568 | tf_op jit(solution)/shard_map/ppermute | solution.py:13
  89.2 1.3 %convolution_convert_fusion.1 = bf16[1024,1024]{1,0:T(8,128)(2,1)S(1)} fusion(bf16[1024,512]{0,1:T(8,128)(2,1)S(1)} %constant_dynamic-update-slice_fusion, bf16[512,1024]{1,0:T(8,128)(2,1)S(1)} %copy-done), kind=kOutput, calls=%fused_computation.17 | convolution fusion | flops 1074790400 | bytes 4194304 | tf_op jit(solution)/shard_map/dot_general | solution.py:17
  92.9 0.5 fusion.47
  94.4 0.6 fusion.138
  95.0 0.7 fusion.139
  95.7 0.6 fusion.140
  96.3 0.7 fusion.141
  97.0 0.6 fusion.142
  97.6 0.7 fusion.143
  98.3 0.6 fusion.144
  99.0 0.7 fusion.137
  99.6 0.6 copy-done.2
  100.2 1.3 %convolution_convert_fusion = bf16[1024,1024]{1,0:T(8,128)(2,1)S(1)} fusion(bf16[1024,512]{0,1:T(8,128)(2,1)S(1)} %constant_dynamic-update-slice_fusion, bf16[512,1024]{1,0:T(8,128)(2,1)S(1)} %copy-done.2), kind=kOutput, calls=%fused_computation.16 | convolution fusion | flops 1074790400 | bytes 4194304 | tf_op jit(solution)/shard_map/dot_general | solution.py:18
  101.5 3.6 %fusion.14 = (f32[512]{0:T(512)S(1)}, f32[512]{0:T(512)S(1)}, f32[512]{0:T(512)S(1)}, f32[512]{0:T(512)S(1)}, f32[512]{0:T(512)S(1)}, /*index=5*/f32[512]{0:T(512)S(1)}, f32[512]{0:T(512)S(1)}, f32[512]{0:T(512)S(1)}) fusion(f32[512,1024]{0,1:T(8,128)S(1)} %get-tuple-element.18, f32[512]{0:T(512)S(1)} %get-tuple-element.17, s32[512]{0:T(512)S(1)} %get-tuple-element.34, ...), kind=kLoop, calls=%fused_computation.32 | loop fusion | flops 13103104 | bytes 16816128 | tf_op jit(solution)/shard_map/reduce_sum | solution.py:57
  105.1 0.6 fusion.64
  105.7 0.6 fusion.65
  106.3 0.6 fusion.66
  106.9 0.6 fusion.67
  107.5 0.6 fusion.68
  108.1 0.6 fusion.69
  108.7 0.6 fusion.70
  109.3 0.6 fusion.71
  109.9 1.3 %copy.8 = bf16[512,1024]{1,0:T(8,128)(2,1)} copy(bf16[512,1024]{0,1:T(8,128)(2,1)S(1)} %fusion.71) | data formatting | bytes 2097152 | tf_op jit(solution)/shard_map/concatenate | solution.py:62
  (19 shorter events, 3.5 us)
Async XLA Ops:
  0.0 89.2 %copy-start = (bf16[512,1024]{1,0:T(8,128)(2,1)S(1)}, bf16[512,1024]{1,0:T(8,128)(2,1)}, u32[]{:S(2)}) copy-start(bf16[512,1024]{1,0:T(8,128)(2,1)} %param.9) | copy-start | bytes 3145732
  0.0 57.6 %collective-permute-start = (s32[2]{0:T(128)}, s32[2]{0:T(128)S(1)}, u32[]{:S(2)}, u32[]{:S(2)}) collective-permute-start(s32[2]{0:T(128)} %param.11), channel_id=1, source_target_pairs={{0,8},{8,16},{16,24},{24,32},{32,40},{40,48},{48,56},{56,64},{64,7... | collective-permute-start | bytes 32 | tf_op jit(solution)/shard_map/ppermute | solution.py:13
  50.2 38.9 %collective-permute-start.1 = (bf16[512,512]{0,1:T(8,128)(2,1)S(1)}, bf16[512,512]{0,1:T(8,128)(2,1)S(1)}, u32[]{:S(2)}, u32[]{:S(2)}) collective-permute-start(bf16[512,512]{0,1:T(8,128)(2,1)S(1)} %all_gather.3), channel_id=1, source_target_pairs={{0,8},{8,16},{16,24},{24,32},{32,40},{40,48},{48,56},{56,64},{64,7... | collective-permute-start | bytes 1572872 | tf_op jit(solution)/shard_map/ppermute | solution.py:13
  52.1 37.0 %collective-permute-start.2 = (bf16[512,64]{0,1:T(8,128)(2,1)}, bf16[512,64]{0,1:T(8,128)(2,1)S(1)}, u32[]{:S(2)}, u32[]{:S(2)}) collective-permute-start(bf16[512,64]{0,1:T(8,128)(2,1)} %param.8), channel_id=1, source_target_pairs={{0,8},{8,16},{16,24},{24,32},{32,40},{40,48},{48,56},{56,64},{64,7... | collective-permute-start | bytes 196616 | tf_op jit(solution)/shard_map/ppermute | solution.py:13
  89.2 1.4 %copy-start.1 = (bf16[512,1536]{1,0:T(8,128)(2,1)S(1)}, bf16[512,1536]{1,0:T(8,128)(2,1)}, u32[]{:S(2)}) copy-start(bf16[512,1536]{1,0:T(8,128)(2,1)} %param.6) | copy-start | bytes 4718596
  99.0 1.2 %copy-start.2 = (bf16[512,1024]{1,0:T(8,128)(2,1)S(1)}, bf16[512,1024]{1,0:T(8,128)(2,1)}, u32[]{:S(2)}) copy-start(bf16[512,1024]{1,0:T(8,128)(2,1)} %param.10) | copy-start | bytes 3145732
where the time goes:
time: 112 us; the launch traced here: 111 us
  blocking collectives  48.1 us (43%)
  waiting for transfers between devices  29.5 us (26%)
  matrix products  16.3 us (15%)
  other arithmetic  6.34 us (6%)
  starting transfers between devices  5.87 us (5%)
  local copies, waits for them, and re-layouts  4.85 us (4%)
    all_gather x1, blocking collectives, shards(): latent_full = lax.all_gather(latent, 'head', axis=1, tiled=True)  48.1 us
    ppermute x3, waiting for transfers between devices, shifted(): lax.ppermute(shard, axis, [(i, (i + by) % peers) for i in range(peers)])  29.5 us
    ppermute x3, starting transfers between devices, shifted(): lax.ppermute(shard, axis, [(i, (i + by) % peers) for i in range(peers)])  5.87 us
    dot_general x8, matrix products, shards(): jnp.einsum('qd,kd->qk', query_rope, rope_all, preferred_element_type=jnp....  5.21 us
    dot_general x8, matrix products, shards(): jnp.dot(weight.astype(jnp.bfloat16), value_head, preferred_element_type=j...  4.73 us
    dot_general x8, matrix products, shards(): jnp.einsum('qd,kd->qk', query_nope, key_head, preferred_element_type=jnp....  3.78 us
    reduce_sum x1, other arithmetic, shards(): total = jnp.sum(weight, axis=-1, keepdims=True)  3.64 us
    mul x2, other arithmetic, positions_of(): return ids_pair[row_ids // half_rows] * half_rows + row_ids % half_rows  2.69 us
  transfers between devices with their start and end apart: 3, of which 1 were waited for; matrix products, arithmetic and copies ran while one was open for 5% of the time, Pallas kernels for 0%

commit v1 on v0

v1 whole, which is shorter than its diff:
```python
import math

import jax
import jax.numpy as jnp
from jax import lax
from jax.experimental import pallas as pl
from jax.experimental.pallas import tpu as pltpu
from jax.sharding import PartitionSpec as P

ROPE = 64
NOPE = 128
VAL = 128
BLOCK = 256
SHARD = 64
ID_ROWS = 16
GAIN = math.log2(math.e) / math.sqrt(NOPE + ROPE)
ORDER = (0, 4, 2, 1, 5, 3, 6, 7)
NEAR = 3
F32 = jnp.float32
BF16 = jnp.bfloat16


def dot(a, b):
    return jnp.dot(a, b, preferred_element_type=F32)


def place(pieces, at, first, lat):
    rows = [(piece, r) for piece in pieces for r in range(0, piece.shape[0], SHARD)]
    other = pl.multiple_of(BLOCK - first, BLOCK)
    for (piece, r), which in zip(rows, ORDER, strict=True):
        to = pl.ds(pl.multiple_of((at ^ which) * SHARD, SHARD), SHARD)
        lat[to, :BLOCK] = piece[r : r + SHARD, pl.ds(first, BLOCK)]
        lat[to, BLOCK:] = piece[r : r + SHARD, pl.ds(other, BLOCK)]


def place_rope(rope_in, first, keys):
    other = pl.multiple_of(BLOCK - first, BLOCK)
    rope = jnp.concatenate([rope_in[:, pl.ds(first, BLOCK)], rope_in[:, pl.ds(other, BLOCK)]], axis=1)
    none = jnp.zeros_like(rope)
    for head in range(keys.shape[0]):
        if head % 2 == 0:
            keys[head, NOPE : NOPE + ROPE, :] = rope
            keys[head, NOPE + ROPE :, :] = none
        else:
            keys[head, :ROPE, :] = none
            keys[head, ROPE + NOPE :, :] = rope


def project(lat, key_up_t, value_up, keys, values):
    features = lat[...]
    for pair in range(keys.shape[0] // 2):
        part = dot(key_up_t[pair * 256 : (pair + 1) * 256, :], features).astype(BF16)
        keys[2 * pair, :NOPE, :] = part[:NOPE]
        keys[2 * pair + 1, ROPE : ROPE + NOPE, :] = part[NOPE:]
    rows = features.T
    for pair in range(keys.shape[0] // 2):
        columns = slice(pair * 256, (pair + 1) * 256)
        values[:, columns] = dot(rows, value_up[:, columns]).astype(BF16)


def own_kernel(ids, queries, a, b, c, d, rope, key_up_t, value_up, acc_out, stat_out, lat, keys, values):
    first = pl.multiple_of(jnp.where(ids[0] < ids[1], 0, BLOCK), BLOCK)
    other = pl.multiple_of(BLOCK - first, BLOCK)
    place((a, b, c, d), lax.axis_index("head"), first, lat)
    place_rope(rope, first, keys)
    project(lat, key_up_t, value_up, keys, values)
    heads = keys.shape[0]
    row = lax.broadcasted_iota(jnp.int32, (BLOCK, BLOCK), 0)
    col = lax.broadcasted_iota(jnp.int32, (BLOCK, BLOCK), 1)
    seen = col <= row
    lane = lax.broadcasted_iota(jnp.int32, (BLOCK, 128), 1)
    stat = [jnp.zeros((BLOCK, 128), F32)] * 2
    ones = jnp.ones((2 * BLOCK, VAL), BF16)
    for head in range(heads):
        base = (head // 2) * 384 + (head % 2) * 128
        columns = slice(head * VAL, (head + 1) * VAL)
        value = jnp.concatenate([values[:, columns], ones], axis=1)
        for part, at in enumerate((first, other)):
            many = BLOCK * (part + 1)
            score = dot(queries[pl.ds(at, BLOCK), base : base + 256], keys[head, :, :many])
            if part == 0:
                score = jnp.where(seen, score, -jnp.inf)
            else:
                score = jnp.concatenate([score[:, :BLOCK], jnp.where(seen, score[:, BLOCK:], -jnp.inf)], axis=1)
            top = jnp.max(score, axis=1, keepdims=True)
            weight = jnp.exp2((score - top) * GAIN).astype(BF16)
            got = dot(weight, value[:many])
            acc_out[pl.ds(at, BLOCK), columns] = got[:, :VAL]
            stat[part] = jnp.where(lane == head, got[:, VAL:], stat[part])
            stat[part] = jnp.where(lane == heads + head, top, stat[part])
    stat_out[pl.ds(first, BLOCK), :] = stat[0]
    stat_out[pl.ds(other, BLOCK), :] = stat[1]


def prior_kernel(ids, queries, near, far, w_near, w_more, w_far, key_up_t, value_up, acc_in, stat_in, out, lat, keys, values, tail):
    turn = lax.axis_size("seq") // 2
    crossing = lax.rem(lax.axis_index("seq"), turn) == 0
    spot = lax.axis_index("head")

    def positions():
        one = jnp.max(tail[ROPE : ROPE + 1, :128].astype(F32)).astype(jnp.int32)
        two = jnp.max(tail[ROPE : ROPE + 1, BLOCK : BLOCK + 128].astype(F32)).astype(jnp.int32)
        return one, two

    def from_chip_beside():
        tail[...] = near[NEAR * SHARD :, :]

    def from_other_half():
        tail[...] = w_near[SHARD:, :]

    pl.when(crossing)(from_other_half)
    pl.when(jnp.logical_not(crossing))(from_chip_beside)
    one, two = positions()
    first = pl.multiple_of(jnp.where(one < two, 0, BLOCK), BLOCK)
    low, high = jnp.minimum(one, two), jnp.maximum(one, two)
    pl.when(crossing)(lambda: place((w_near.at[:SHARD], *w_more, *w_far), spot ^ 7, first, lat))
    pl.when(jnp.logical_not(crossing))(lambda: place((near.at[: NEAR * SHARD], far), spot, first, lat))
    place_rope(tail.at[:ROPE], first, keys)
    project(lat, key_up_t, value_up, keys, values)
    heads = keys.shape[0]
    ones = jnp.ones((2 * BLOCK, VAL), BF16)

    def merged(part, many):
        def body():
            for head in range(heads):
                base = (head // 2) * 384 + (head % 2) * 128
                rows = pl.ds(part * BLOCK, BLOCK)
                columns = slice(head * VAL, (head + 1) * VAL)
                total = stat_in[rows, head : head + 1]
                if many == 0:
                    out[rows, columns] = (acc_in[rows, columns] / total).astype(BF16)
                    continue
                value = jnp.concatenate([values[:many, columns], ones[:many]], axis=1)
                score = dot(queries[rows, base : base + 256], keys[head, :, :many])
                before = stat_in[rows, heads + head : heads + head + 1]
                top = jnp.maximum(before, jnp.max(score, axis=1, keepdims=True))
                weight = jnp.exp2((score - top) * GAIN).astype(BF16)
                keep = jnp.exp2((before - top) * GAIN)
                got = dot(weight, value)
                total = got[:, VAL:] + total * keep
                out[rows, columns] = ((got[:, :VAL] + acc_in[rows, columns] * keep) / total).astype(BF16)

        return body

    for part in range(2):
        mine = ids[part]
        count = (low <= mine).astype(jnp.int32) + (high <= mine).astype(jnp.int32)
        for many in range(3):
            pl.when(count == many)(merged(part, many * BLOCK))


VMEM = pl.BlockSpec(memory_space=pltpu.VMEM)
SMEM = pl.BlockSpec(memory_space=pltpu.SMEM)


def scratch_of(tokens, heads, features):
    return [
        pltpu.VMEM((features, tokens), BF16),
        pltpu.VMEM((heads, 256, tokens), BF16),
        pltpu.VMEM((tokens, heads * VAL), BF16),
    ]


def own_part(ids, queries, pieces, rope, key_up_t, value_up):
    tokens, heads = queries.shape[0], value_up.shape[1] // VAL
    return pl.pallas_call(
        own_kernel,
        out_shape=(jax.ShapeDtypeStruct((tokens, heads * VAL), F32), jax.ShapeDtypeStruct((tokens, 128), F32)),
        in_specs=[SMEM] + [VMEM] * 8,
        out_specs=(VMEM, VMEM),
        scratch_shapes=scratch_of(tokens, heads, value_up.shape[0]),
        compiler_params=pltpu.CompilerParams(vmem_limit_bytes=40 << 20),
        cost_estimate=pl.CostEstimate(flops=3 << 30, bytes_accessed=8 << 20, transcendentals=1 << 21),
        name="own_part",
    )(ids, queries, *pieces, rope, key_up_t, value_up)


def prior_part(ids, queries, near, far, w_near, w_more, w_far, key_up_t, value_up, acc, stat):
    tokens, heads = queries.shape[0], value_up.shape[1] // VAL

    def kernel(ids, queries, near, far, w_near, wa, wb, wc, wd, we, *rest):
        prior_kernel(ids, queries, near, far, w_near, (wa, wb), (wc, wd, we), *rest)

    return pl.pallas_call(
        kernel,
        out_shape=jax.ShapeDtypeStruct((tokens, heads * VAL), BF16),
        in_specs=[SMEM] + [VMEM] * 13,
        out_specs=VMEM,
        scratch_shapes=scratch_of(tokens, heads, value_up.shape[0]) + [pltpu.VMEM((ROPE + ID_ROWS, tokens), BF16)],
        compiler_params=pltpu.CompilerParams(vmem_limit_bytes=40 << 20),
        cost_estimate=pl.CostEstimate(flops=4 << 30, bytes_accessed=8 << 20, transcendentals=1 << 21),
        name="prior_part",
    )(ids, queries, near, far, w_near, *w_more, *w_far, key_up_t, value_up, acc, stat)


def swapped(shard, by):
    return lax.ppermute(shard, "head", [(i, i ^ by) for i in range(lax.axis_size("head"))])


def joined(*parts):
    return jnp.concatenate(parts, axis=0)


def shards(queries, latent, key_rope, key_up, value_up, block_ids):
    groups, peers = lax.axis_size("seq"), lax.axis_size("head")
    turn = groups // 2
    both = ("seq", "head")
    tokens = queries.shape[0]

    def beside(shard):
        return lax.ppermute(shard, "seq", [(i, i + 1) for i in range(groups) if (i + 1) % turn])

    def across(shard, by):
        pairs = [(i, (i + 1) % groups) for i in range(turn - 1, groups, turn)]
        return lax.ppermute(shard, both, [(s * peers + (h ^ by), t * peers + h) for s, t in pairs for h in range(peers)])

    def swapped_there(shard, by):
        return lax.ppermute(shard, both, [(t * peers + (h ^ by), t * peers + h) for t in range(0, groups, turn) for h in range(peers)])

    mine, rope = latent.T, key_rope.T
    id_row = jnp.repeat(block_ids.astype(BF16), tokens // 2)
    tail = joined(rope, jnp.broadcast_to(id_row[None], (ID_ROWS, tokens)))
    by4, by2 = swapped(mine, 4), swapped(mine, 2)
    w_near = across(joined(mine, tail), 7)
    w_more = (across(mine, 3), across(mine, 5))
    held = joined(mine, by4, by2)
    got = (swapped(held, 1), swapped(by4, 2), swapped(by4, 3))
    near = beside(joined(held, tail))
    w_far = (swapped_there(joined(w_near[:SHARD], *w_more), 1), swapped_there(w_more[0], 2), swapped_there(w_more[0], 3))
    far = beside(joined(*got))
    key_up_t = key_up.T
    acc, stat = own_part(block_ids, queries, (held, *got), rope, key_up_t, value_up)
    return prior_part(block_ids, queries, near, far, w_near, w_more, w_far, key_up_t, value_up, acc, stat)


def solution(mesh):
    in_specs = (
        P("seq", "head"),
        P("seq", "head"),
        P("seq", None),
        P(None, "head"),
        P(None, "head"),
        P("seq"),
    )
    out_specs = P("seq", "head")
    return jax.shard_map(shards, mesh=mesh, in_specs=in_specs, out_specs=out_specs, check_vma=False)
```

time: 112 us -> 69.4 us (0.62)
  the two profiles are of different devices: /device:TPU:0 before, /device:TPU:32 now
where the time goes in v1:
time: 69.4 us; the launch traced here: 68.8 us
  starting transfers between devices  38.2 us (55%)
  Pallas kernels  15.5 us (22%)
  waiting for transfers between devices  9.55 us (14%)
  local copies, waits for them, and re-layouts  3.7 us (5%)
  other arithmetic  1.6 us (2%)
    ppermute x5, starting transfers between devices, swapped(): lax.ppermute(shard, 'head', [(i, i ^ by) for i in range(lax.axis_size('he...  24.4 us
    pallas_call x1, Pallas kernels, prior_part(): pl.pallas_call(kernel, out_shape=jax.ShapeDtypeStruct((tokens, heads * VA...  10.6 us
    ppermute x3, waiting for transfers between devices, across(): lax.ppermute(shard, both, [(s * peers + (h ^ by), t * peers + h) for s, t...  9.53 us
    ppermute x3, starting transfers between devices, swapped_there(): lax.ppermute(shard, both, [(t * peers + (h ^ by), t * peers + h) for t in...  7.05 us
    pallas_call x1, Pallas kernels, own_part(): pl.pallas_call(own_kernel, out_shape=(jax.ShapeDtypeStruct((tokens, heads...  4.87 us
    ppermute x3, starting transfers between devices, across(): lax.ppermute(shard, both, [(s * peers + (h ^ by), t * peers + h) for s, t...  4.12 us
    unnamed x17, local copies, waits for them, and re-layouts  3.68 us
    ppermute x2, starting transfers between devices, beside(): lax.ppermute(shard, 'seq', [(i, i + 1) for i in range(groups) if (i + 1)...  2.62 us
  transfers between devices with their start and end apart: 13, of which 2 were waited for; matrix products, arithmetic and copies ran while one was open for 6% of the time, Pallas kernels for 7%

profile of v1, /device:TPU:32, one launch (start us, length us, event | category | flops | bytes accessed | tf_op | source)
XLA Modules:
  0.0 68.8 jit_solution(15319612451992262236)
XLA Ops:
  0.0 1.4 %collective-permute-start.8 = (bf16[64,512]{1,0:T(8,128)(2,1)}, bf16[64,512]{1,0:T(8,128)(2,1)S(1)}, u32[]{:S(2)}, u32[]{:S(2)}) collective-permute-start(bf16[64,512]{1,0:T(8,128)(2,1)} %bitcast.12), channel_id=1, source_target_pairs={{251,256},{250,257},{249,258},{248,259},{255,260},{254,261},{253,2... | collective-permute-start | bytes 196616 | tf_op jit(solution)/shard_map/ppermute | solution.py:215
  1.4 5.2 %collective-permute-start.1 = (bf16[64,512]{1,0:T(8,128)(2,1)}, bf16[64,512]{1,0:T(8,128)(2,1)S(1)}, u32[]{:S(2)}, u32[]{:S(2)}) collective-permute-start(bf16[64,512]{1,0:T(8,128)(2,1)} %bitcast.13), channel_id=1, source_target_pairs={{0,2},{1,3},{2,0},{3,1},{4,6},{5,7},{6,4},{7,5},{8,10},{9,11},{10,... | collective-permute-start | bytes 196616 | tf_op jit(solution)/shard_map/ppermute | solution.py:197
  6.6 9.1 %collective-permute-start = (bf16[64,512]{1,0:T(8,128)(2,1)}, bf16[64,512]{1,0:T(8,128)(2,1)S(1)}, u32[]{:S(2)}, u32[]{:S(2)}) collective-permute-start(bf16[64,512]{1,0:T(8,128)(2,1)} %bitcast.14), channel_id=1, source_target_pairs={{0,4},{1,5},{2,6},{3,7},{4,0},{5,1},{6,2},{7,3},{8,12},{9,13},{10,... | collective-permute-start | bytes 196616 | tf_op jit(solution)/shard_map/ppermute | solution.py:197
  15.7 0.7 convert_element_type.3
  16.4 0.1 broadcast_bitcast_fusion
  16.5 0.9 %pad_maximum_fusion.3 = bf16[144,512]{1,0:T(8,128)(2,1)S(1)} fusion(bf16[16,512]{1,0:T(8,128)(2,1)S(1)} %broadcast_in_dim.12, bf16[64,512]{1,0:T(8,128)(2,1)} %bitcast.10, bf16[64,512]{1,0:T(8,128)(2,1)} %bitcast.15), kind=kLoop, calls=%fused_computation.3 | loop fusion | flops 442368 | bytes 294912 | tf_op jit(solution)/shard_map/concatenate | solution.py:201
  17.4 0.0 copy-start.1
  17.4 0.0 copy-start.3
  17.4 1.4 %collective-permute-start.7 = (bf16[144,512]{1,0:T(8,128)(2,1)S(1)}, bf16[144,512]{1,0:T(8,128)(2,1)S(1)}, u32[]{:S(2)}, u32[]{:S(2)}) collective-permute-start(bf16[144,512]{1,0:T(8,128)(2,1)S(1)} %pad_maximum_fusion.3), channel_id=1, source_target_pairs={{255,256},{254,257},{253,258},{252,259},{251,260},{250,261},{249,2... | collective-permute-start | bytes 442376 | tf_op jit(solution)/shard_map/ppermute | solution.py:215
  18.8 0.8 %constant_dynamic-update-slice_fusion.4 = bf16[272,512]{1,0:T(8,128)(2,1)S(1)} fusion(bf16[512,64]{0,1:T(8,128)(2,1)} %param.7), kind=kLoop, calls=%fused_computation.8 | loop fusion | bytes 131072
  19.7 1.5 %copy.7 = bf16[512,1024]{0,1:T(8,128)(2,1)S(1)} copy(bf16[512,1024]{1,0:T(8,128)(2,1)} %param.9) | data formatting | bytes 2097152 | tf_op args[3]
  21.2 0.0 collective-permute-done.1
  21.2 0.0 collective-permute-done
  21.2 2.4 %collective-permute-start.3 = (bf16[192,512]{1,0:T(8,128)(2,1)S(1)}, bf16[192,512]{1,0:T(8,128)(2,1)S(1)}, u32[]{:S(2)}, u32[]{:S(2)}) collective-permute-start(bf16[192,512]{1,0:T(8,128)(2,1)S(1)} %pad_maximum_fusion.1.a), channel_id=1, source_target_pairs={{0,1},{1,0},{2,3},{3,2},{4,5},{5,4},{6,7},{7,6},{8,9},{9,8},{10,11... | collective-permute-start | bytes 589832 | tf_op jit(solution)/shard_map/ppermute | solution.py:197
  23.7 2.0 %collective-permute-start.5 = (bf16[64,512]{1,0:T(8,128)(2,1)S(1)}, bf16[64,512]{1,0:T(8,128)(2,1)S(1)}, u32[]{:S(2)}, u32[]{:S(2)}) collective-permute-start(bf16[64,512]{1,0:T(8,128)(2,1)S(1)} %collective-permute-done), channel_id=1, source_target_pairs={{0,3},{1,2},{2,1},{3,0},{4,7},{5,6},{6,5},{7,4},{8,11},{9,10},{10,... | collective-permute-start | bytes 196616 | tf_op jit(solution)/shard_map/ppermute | solution.py:197
  25.7 5.7 %collective-permute-start.4 = (bf16[64,512]{1,0:T(8,128)(2,1)S(1)}, bf16[64,512]{1,0:T(8,128)(2,1)S(1)}, u32[]{:S(2)}, u32[]{:S(2)}) collective-permute-start(bf16[64,512]{1,0:T(8,128)(2,1)S(1)} %collective-permute-done), channel_id=1, source_target_pairs={{0,2},{1,3},{2,0},{3,1},{4,6},{5,7},{6,4},{7,5},{8,10},{9,11},{10,... | collective-permute-start | bytes 196616 | tf_op jit(solution)/shard_map/ppermute | solution.py:197
  31.4 4.1 %collective-permute-done.7.w_near = bf16[144,512]{1,0:T(8,128)(2,1)S(1)} collective-permute-done((bf16[144,512]{1,0:T(8,128)(2,1)S(1)}, bf16[144,512]{1,0:T(8,128)(2,1)S(1)}, u32[]{:S(2)}, u32[]{:S(2)}) %collective-permute-start.7) | collective-permute-done | bytes 147488 | tf_op jit(solution)/shard_map/ppermute | solution.py:215
  35.5 1.3 %collective-permute-start.9 = (bf16[64,512]{1,0:T(8,128)(2,1)S(1)}, bf16[64,512]{1,0:T(8,128)(2,1)S(1)}, u32[]{:S(2)}, u32[]{:S(2)}) collective-permute-start(bf16[64,512]{1,0:T(8,128)(2,1)S(1)} %bitcast.17), channel_id=1, source_target_pairs={{253,256},{252,257},{255,258},{254,259},{249,260},{248,261},{251,2... | collective-permute-start | bytes 196616 | tf_op jit(solution)/shard_map/ppermute | solution.py:215
  36.8 1.3 %collective-permute-start.2 = (bf16[272,512]{1,0:T(8,128)(2,1)S(1)}, bf16[272,512]{1,0:T(8,128)(2,1)S(1)}, u32[]{:S(2)}, u32[]{:S(2)}) collective-permute-start(bf16[272,512]{1,0:T(8,128)(2,1)S(1)} %constant_dynamic-update-slice_fusion), channel_id=1, source_target_pairs={{0,8},{8,16},{16,24},{24,32},{32,40},{40,48},{48,56},{56,64},{64,7... | collective-permute-start | bytes 835592 | tf_op jit(solution)/shard_map/ppermute | solution.py:211
  38.1 3.0 %collective-permute-start.12 = (bf16[64,512]{1,0:T(8,128)(2,1)S(1)}, bf16[64,512]{1,0:T(8,128)(2,1)S(1)}, u32[]{:S(2)}, u32[]{:S(2)}) collective-permute-start(bf16[64,512]{1,0:T(8,128)(2,1)S(1)} %collective-permute-done.8.wa), channel_id=1, source_target_pairs={{3,0},{2,1},{1,2},{0,3},{7,4},{6,5},{5,6},{4,7},{259,256},{258,257... | collective-permute-start | bytes 196616 | tf_op jit(solution)/shard_map/ppermute | solution.py:218
  41.2 2.1 %collective-permute-start.11 = (bf16[64,512]{1,0:T(8,128)(2,1)S(1)}, bf16[64,512]{1,0:T(8,128)(2,1)S(1)}, u32[]{:S(2)}, u32[]{:S(2)}) collective-permute-start(bf16[64,512]{1,0:T(8,128)(2,1)S(1)} %collective-permute-done.8.wa), channel_id=1, source_target_pairs={{2,0},{3,1},{0,2},{1,3},{6,4},{7,5},{4,6},{5,7},{258,256},{259,257... | collective-permute-start | bytes 196616 | tf_op jit(solution)/shard_map/ppermute | solution.py:218
  43.3 0.0 collective-permute-done.3.b
  43.3 1.3 %collective-permute-start.6 = (bf16[320,512]{1,0:T(8,128)(2,1)S(1)}, bf16[320,512]{1,0:T(8,128)(2,1)S(1)}, u32[]{:S(2)}, u32[]{:S(2)}) collective-permute-start(bf16[320,512]{1,0:T(8,128)(2,1)S(1)} %pad_maximum_fusion), channel_id=1, source_target_pairs={{0,8},{8,16},{16,24},{24,32},{32,40},{40,48},{48,56},{56,64},{64,7... | collective-permute-start | bytes 983048 | tf_op jit(solution)/shard_map/ppermute | solution.py:211
  44.7 5.4 %collective-permute-done.9.wb = bf16[64,512]{1,0:T(8,128)(2,1)S(1)} collective-permute-done((bf16[64,512]{1,0:T(8,128)(2,1)S(1)}, bf16[64,512]{1,0:T(8,128)(2,1)S(1)}, u32[]{:S(2)}, u32[]{:S(2)}) %collective-permute-start.9) | collective-permute-done | bytes 65568 | tf_op jit(solution)/shard_map/ppermute | solution.py:215
  50.1 1.9 %collective-permute-start.10 = (bf16[192,512]{1,0:T(8,128)(2,1)S(1)}, bf16[192,512]{1,0:T(8,128)(2,1)S(1)}, u32[]{:S(2)}, u32[]{:S(2)}) collective-permute-start(bf16[192,512]{1,0:T(8,128)(2,1)S(1)} %pad_maximum_fusion.2), channel_id=1, source_target_pairs={{1,0},{0,1},{3,2},{2,3},{5,4},{4,5},{7,6},{6,7},{257,256},{256,257... | collective-permute-start | bytes 589832 | tf_op jit(solution)/shard_map/ppermute | solution.py:218
  52.1 0.0 copy-start.2
  52.1 1.2 %copy-done.2 = bf16[512,1024]{1,0:T(8,128)(2,1)S(1)} copy-done((bf16[512,1024]{1,0:T(8,128)(2,1)S(1)}, bf16[512,1024]{1,0:T(8,128)(2,1)}, u32[]{:S(2)}) %copy-start.2) | copy-done | bytes 1048600
  53.3 4.9 %own_part.1 = (f32[512,1024]{1,0:T(8,128)S(1)}, f32[512,128]{1,0:T(8,128)S(1)}) custom-call(s32[2]{0:T(128)S(1)} %copy-done.3, bf16[512,1536]{1,0:T(8,128)(2,1)S(1)} %copy-done.1, bf16[192,512]{1,0:T(8,128)(2,1)S(1)} %pad_maximum_fusion.1.a, bf16[192,512]{1,0:T(8,128)(2,1)S(1)} %collective-permute-done.3.b, bf16[64,512]{1,0:T(8,128)(2,1)S(1)} %collective-permute-done.4.c, ...), custom_call_target="tpu_custom_call" | custom-call | flops 3221225472 | bytes 8388608 | tf_op jit(solution)/shard_map/own_part/pallas_call | solution.py:166
  58.2 0.0 collective-permute-done.12.we
  58.2 0.0 collective-permute-done.10.wc
  58.2 0.0 collective-permute-done.2.near
  58.2 10.6 %prior_part.1 = bf16[512,1024]{1,0:T(8,128)(2,1)} custom-call(s32[2]{0:T(128)S(1)} %copy-done.3, bf16[512,1536]{1,0:T(8,128)(2,1)S(1)} %copy-done.1, bf16[272,512]{1,0:T(8,128)(2,1)S(1)} %collective-permute-done.2.near, bf16[320,512]{1,0:T(8,128)(2,1)S(1)} %collective-permute-done.6.far, bf16[144,512]{1,0:T(8,128)(2,1)S(1)} %collective-permute-done.7.w_near, ...), custom_call_target="tpu_custom_call" | custom-call | flops 4294967296 | bytes 8388608 | tf_op jit(solution)/shard_map/prior_part/pallas_call | solution.py:184
  (21 shorter events, 0.1 us)
Async XLA Ops:
  0.0 21.2 %copy-start.4 = (bf16[512,64]{0,1:T(8,128)(2,1)S(1)}, bf16[512,64]{0,1:T(8,128)(2,1)}, u32[]{:S(2)}) copy-start(bf16[512,64]{0,1:T(8,128)(2,1)} %param.7) | copy-start | bytes 196612
  0.0 23.7 %copy-start = (bf16[512,64]{0,1:T(8,128)(2,1)S(1)}, bf16[512,64]{0,1:T(8,128)(2,1)}, u32[]{:S(2)}) copy-start(bf16[512,64]{0,1:T(8,128)(2,1)} %param.8) | copy-start | bytes 196612
  0.0 36.8 %collective-permute-start.8 = (bf16[64,512]{1,0:T(8,128)(2,1)}, bf16[64,512]{1,0:T(8,128)(2,1)S(1)}, u32[]{:S(2)}, u32[]{:S(2)}) collective-permute-start(bf16[64,512]{1,0:T(8,128)(2,1)} %bitcast.12), channel_id=1, source_target_pairs={{251,256},{250,257},{249,258},{248,259},{255,260},{254,261},{253,2... | collective-permute-start | bytes 196616 | tf_op jit(solution)/shard_map/ppermute | solution.py:215
  1.4 19.7 %collective-permute-start.1 = (bf16[64,512]{1,0:T(8,128)(2,1)}, bf16[64,512]{1,0:T(8,128)(2,1)S(1)}, u32[]{:S(2)}, u32[]{:S(2)}) collective-permute-start(bf16[64,512]{1,0:T(8,128)(2,1)} %bitcast.13), channel_id=1, source_target_pairs={{0,2},{1,3},{2,0},{3,1},{4,6},{5,7},{6,4},{7,5},{8,10},{9,11},{10,... | collective-permute-start | bytes 196616 | tf_op jit(solution)/shard_map/ppermute | solution.py:197
  6.6 14.6 %collective-permute-start = (bf16[64,512]{1,0:T(8,128)(2,1)}, bf16[64,512]{1,0:T(8,128)(2,1)S(1)}, u32[]{:S(2)}, u32[]{:S(2)}) collective-permute-start(bf16[64,512]{1,0:T(8,128)(2,1)} %bitcast.14), channel_id=1, source_target_pairs={{0,4},{1,5},{2,6},{3,7},{4,0},{5,1},{6,2},{7,3},{8,12},{9,13},{10,... | collective-permute-start | bytes 196616 | tf_op jit(solution)/shard_map/ppermute | solution.py:197
  17.4 34.7 %copy-start.1 = (bf16[512,1536]{1,0:T(8,128)(2,1)S(1)}, bf16[512,1536]{1,0:T(8,128)(2,1)}, u32[]{:S(2)}) copy-start(bf16[512,1536]{1,0:T(8,128)(2,1)} %queries.3) | copy-start | bytes 4718596
  17.4 34.7 %copy-start.3 = (s32[2]{0:T(128)S(1)}, s32[2]{0:T(128)}, u32[]{:S(2)}) copy-start(s32[2]{0:T(128)} %ids.3) | copy-start | bytes 28
  17.4 18.1 %collective-permute-start.7 = (bf16[144,512]{1,0:T(8,128)(2,1)S(1)}, bf16[144,512]{1,0:T(8,128)(2,1)S(1)}, u32[]{:S(2)}, u32[]{:S(2)}) collective-permute-start(bf16[144,512]{1,0:T(8,128)(2,1)S(1)} %pad_maximum_fusion.3), channel_id=1, source_target_pairs={{255,256},{254,257},{253,258},{252,259},{251,260},{250,261},{249,2... | collective-permute-start | bytes 442376 | tf_op jit(solution)/shard_map/ppermute | solution.py:215
  21.2 22.1 %collective-permute-start.3 = (bf16[192,512]{1,0:T(8,128)(2,1)S(1)}, bf16[192,512]{1,0:T(8,128)(2,1)S(1)}, u32[]{:S(2)}, u32[]{:S(2)}) collective-permute-start(bf16[192,512]{1,0:T(8,128)(2,1)S(1)} %pad_maximum_fusion.1.a), channel_id=1, source_target_pairs={{0,1},{1,0},{2,3},{3,2},{4,5},{5,4},{6,7},{7,6},{8,9},{9,8},{10,11... | collective-permute-start | bytes 589832 | tf_op jit(solution)/shard_map/ppermute | solution.py:197
  23.7 14.4 %collective-permute-start.5 = (bf16[64,512]{1,0:T(8,128)(2,1)S(1)}, bf16[64,512]{1,0:T(8,128)(2,1)S(1)}, u32[]{:S(2)}, u32[]{:S(2)}) collective-permute-start(bf16[64,512]{1,0:T(8,128)(2,1)S(1)} %collective-permute-done), channel_id=1, source_target_pairs={{0,3},{1,2},{2,1},{3,0},{4,7},{5,6},{6,5},{7,4},{8,11},{9,10},{10,... | collective-permute-start | bytes 196616 | tf_op jit(solution)/shard_map/ppermute | solution.py:197
  25.7 15.5 %collective-permute-start.4 = (bf16[64,512]{1,0:T(8,128)(2,1)S(1)}, bf16[64,512]{1,0:T(8,128)(2,1)S(1)}, u32[]{:S(2)}, u32[]{:S(2)}) collective-permute-start(bf16[64,512]{1,0:T(8,128)(2,1)S(1)} %collective-permute-done), channel_id=1, source_target_pairs={{0,2},{1,3},{2,0},{3,1},{4,6},{5,7},{6,4},{7,5},{8,10},{9,11},{10,... | collective-permute-start | bytes 196616 | tf_op jit(solution)/shard_map/ppermute | solution.py:197
  35.5 14.6 %collective-permute-start.9 = (bf16[64,512]{1,0:T(8,128)(2,1)S(1)}, bf16[64,512]{1,0:T(8,128)(2,1)S(1)}, u32[]{:S(2)}, u32[]{:S(2)}) collective-permute-start(bf16[64,512]{1,0:T(8,128)(2,1)S(1)} %bitcast.17), channel_id=1, source_target_pairs={{253,256},{252,257},{255,258},{254,259},{249,260},{248,261},{251,2... | collective-permute-start | bytes 196616 | tf_op jit(solution)/shard_map/ppermute | solution.py:215
  36.8 21.4 %collective-permute-start.2 = (bf16[272,512]{1,0:T(8,128)(2,1)S(1)}, bf16[272,512]{1,0:T(8,128)(2,1)S(1)}, u32[]{:S(2)}, u32[]{:S(2)}) collective-permute-start(bf16[272,512]{1,0:T(8,128)(2,1)S(1)} %constant_dynamic-update-slice_fusion), channel_id=1, source_target_pairs={{0,8},{8,16},{16,24},{24,32},{32,40},{40,48},{48,56},{56,64},{64,7... | collective-permute-start | bytes 835592 | tf_op jit(solution)/shard_map/ppermute | solution.py:211
  38.1 20.0 %collective-permute-start.12 = (bf16[64,512]{1,0:T(8,128)(2,1)S(1)}, bf16[64,512]{1,0:T(8,128)(2,1)S(1)}, u32[]{:S(2)}, u32[]{:S(2)}) collective-permute-start(bf16[64,512]{1,0:T(8,128)(2,1)S(1)} %collective-permute-done.8.wa), channel_id=1, source_target_pairs={{3,0},{2,1},{1,2},{0,3},{7,4},{6,5},{5,6},{4,7},{259,256},{258,257... | collective-permute-start | bytes 196616 | tf_op jit(solution)/shard_map/ppermute | solution.py:218
  41.2 17.0 %collective-permute-start.11 = (bf16[64,512]{1,0:T(8,128)(2,1)S(1)}, bf16[64,512]{1,0:T(8,128)(2,1)S(1)}, u32[]{:S(2)}, u32[]{:S(2)}) collective-permute-start(bf16[64,512]{1,0:T(8,128)(2,1)S(1)} %collective-permute-done.8.wa), channel_id=1, source_target_pairs={{2,0},{3,1},{0,2},{1,3},{6,4},{7,5},{4,6},{5,7},{258,256},{259,257... | collective-permute-start | bytes 196616 | tf_op jit(solution)/shard_map/ppermute | solution.py:218
  43.3 14.9 %collective-permute-start.6 = (bf16[320,512]{1,0:T(8,128)(2,1)S(1)}, bf16[320,512]{1,0:T(8,128)(2,1)S(1)}, u32[]{:S(2)}, u32[]{:S(2)}) collective-permute-start(bf16[320,512]{1,0:T(8,128)(2,1)S(1)} %pad_maximum_fusion), channel_id=1, source_target_pairs={{0,8},{8,16},{16,24},{24,32},{32,40},{40,48},{48,56},{56,64},{64,7... | collective-permute-start | bytes 983048 | tf_op jit(solution)/shard_map/ppermute | solution.py:211
  50.1 8.1 %collective-permute-start.10 = (bf16[192,512]{1,0:T(8,128)(2,1)S(1)}, bf16[192,512]{1,0:T(8,128)(2,1)S(1)}, u32[]{:S(2)}, u32[]{:S(2)}) collective-permute-start(bf16[192,512]{1,0:T(8,128)(2,1)S(1)} %pad_maximum_fusion.2), channel_id=1, source_target_pairs={{1,0},{0,1},{3,2},{2,3},{5,4},{4,5},{7,6},{6,7},{257,256},{256,257... | collective-permute-start | bytes 589832 | tf_op jit(solution)/shard_map/ppermute | solution.py:218
  52.1 1.2 %copy-start.2 = (bf16[512,1024]{1,0:T(8,128)(2,1)S(1)}, bf16[512,1024]{1,0:T(8,128)(2,1)}, u32[]{:S(2)}) copy-start(bf16[512,1024]{1,0:T(8,128)(2,1)} %rest_1_.1) | copy-start | bytes 3145732

commit v2 on v1

--- a/solution.py
+++ b/solution.py
@@ -14,8 +14,8 @@
 SHARD = 64
 ID_ROWS = 16
 GAIN = math.log2(math.e) / math.sqrt(NOPE + ROPE)
-ORDER = (0, 4, 2, 1, 5, 3, 6, 7)
-NEAR = 3
+ORDER = (0, 4, 1, 5, 2, 6, 3, 7)
+NEAR = 2
 F32 = jnp.float32
 BF16 = jnp.bfloat16
 
@@ -58,7 +58,7 @@
         values[:, columns] = dot(rows, value_up[:, columns]).astype(BF16)
 
 
-def own_kernel(ids, queries, a, b, c, d, rope, key_up_t, value_up, acc_out, stat_out, lat, keys, values):
+def own_kernel(ids, queries, a, b, c, d, rope, key_up_t, value_up, acc_out, sum_out, top_out, lat, keys, values):
     first = pl.multiple_of(jnp.where(ids[0] < ids[1], 0, BLOCK), BLOCK)
     other = pl.multiple_of(BLOCK - first, BLOCK)
     place((a, b, c, d), lax.axis_index("head"), first, lat)
@@ -68,16 +68,21 @@
     row = lax.broadcasted_iota(jnp.int32, (BLOCK, BLOCK), 0)
     col = lax.broadcasted_iota(jnp.int32, (BLOCK, BLOCK), 1)
     seen = col <= row
-    lane = lax.broadcasted_iota(jnp.int32, (BLOCK, 128), 1)
-    stat = [jnp.zeros((BLOCK, 128), F32)] * 2
     ones = jnp.ones((2 * BLOCK, VAL), BF16)
+    def scores(head):
+        base = (head // 2) * 384 + (head % 2) * 128
+        return [dot(queries[pl.ds(at, BLOCK), base : base + 256], keys[head, :, : BLOCK * (part + 1)]) for part, at in enumerate((first, other))]
+
+    ahead = scores(0)
     for head in range(heads):
-        base = (head // 2) * 384 + (head % 2) * 128
+        now = ahead
+        if head + 1 < heads:
+            ahead = scores(head + 1)
         columns = slice(head * VAL, (head + 1) * VAL)
         value = jnp.concatenate([values[:, columns], ones], axis=1)
         for part, at in enumerate((first, other)):
             many = BLOCK * (part + 1)
-            score = dot(queries[pl.ds(at, BLOCK), base : base + 256], keys[head, :, :many])
+            score = now[part]
             if part == 0:
                 score = jnp.where(seen, score, -jnp.inf)
             else:
@@ -86,13 +91,11 @@
             weight = jnp.exp2((score - top) * GAIN).astype(BF16)
             got = dot(weight, value[:many])
             acc_out[pl.ds(at, BLOCK), columns] = got[:, :VAL]
-            stat[part] = jnp.where(lane == head, got[:, VAL:], stat[part])
-            stat[part] = jnp.where(lane == heads + head, top, stat[part])
-    stat_out[pl.ds(first, BLOCK), :] = stat[0]
-    stat_out[pl.ds(other, BLOCK), :] = stat[1]
-
-
-def prior_kernel(ids, queries, near, far, w_near, w_more, w_far, key_up_t, value_up, acc_in, stat_in, out, lat, keys, values, tail):
+            sum_out[pl.ds(at, BLOCK), columns] = got[:, VAL:]
+            top_out[pl.ds(at, BLOCK), columns] = jnp.broadcast_to(top, (BLOCK, VAL))
+
+
+def prior_kernel(ids, queries, near, far, w_near, w_more, w_far, key_up_t, value_up, acc_in, sum_in, top_in, out, lat, keys, values, tail):
     turn = lax.axis_size("seq") // 2
     crossing = lax.rem(lax.axis_index("seq"), turn) == 0
     spot = lax.axis_index("head")
@@ -120,33 +123,43 @@
     heads = keys.shape[0]
     ones = jnp.ones((2 * BLOCK, VAL), BF16)
 
-    def merged(part, many):
+    def merged(start, size, many):
+        rows = slice(start, start + size)
+
+        def scores(head):
+            base = (head // 2) * 384 + (head % 2) * 128
+            return dot(queries[rows, base : base + 256], keys[head, :, :many])
+
         def body():
+            ahead = scores(0)
             for head in range(heads):
-                base = (head // 2) * 384 + (head % 2) * 128
-                rows = pl.ds(part * BLOCK, BLOCK)
+                score = ahead
+                if head + 1 < heads:
+                    ahead = scores(head + 1)
                 columns = slice(head * VAL, (head + 1) * VAL)
-                total = stat_in[rows, head : head + 1]
-                if many == 0:
-                    out[rows, columns] = (acc_in[rows, columns] / total).astype(BF16)
-                    continue
                 value = jnp.concatenate([values[:many, columns], ones[:many]], axis=1)
-                score = dot(queries[rows, base : base + 256], keys[head, :, :many])
-                before = stat_in[rows, heads + head : heads + head + 1]
+                before = top_in[rows, columns]
                 top = jnp.maximum(before, jnp.max(score, axis=1, keepdims=True))
-                weight = jnp.exp2((score - top) * GAIN).astype(BF16)
+                weight = jnp.exp2((score - jnp.concatenate([top] * (many // VAL), axis=1)) * GAIN).astype(BF16)
                 keep = jnp.exp2((before - top) * GAIN)
                 got = dot(weight, value)
-                total = got[:, VAL:] + total * keep
+                total = got[:, VAL:] + sum_in[rows, columns] * keep
                 out[rows, columns] = ((got[:, :VAL] + acc_in[rows, columns] * keep) / total).astype(BF16)
 
         return body
 
+    def alone(start):
+        rows = slice(start, start + BLOCK)
+        return lambda: out.__setitem__((rows, slice(None)), (acc_in[rows, :] / sum_in[rows, :]).astype(BF16))
+
+    counts = [(low <= ids[part]).astype(jnp.int32) + (high <= ids[part]).astype(jnp.int32) for part in range(2)]
+    whole = jnp.logical_and(counts[0] == 2, counts[1] == 2)
+    pl.when(whole)(merged(0, 2 * BLOCK, 2 * BLOCK))
     for part in range(2):
-        mine = ids[part]
-        count = (low <= mine).astype(jnp.int32) + (high <= mine).astype(jnp.int32)
-        for many in range(3):
-            pl.when(count == many)(merged(part, many * BLOCK))
+        start = part * BLOCK
+        pl.when(counts[part] == 0)(alone(start))
+        pl.when(counts[part] == 1)(merged(start, BLOCK, BLOCK))
+        pl.when(jnp.logical_and(counts[part] == 2, jnp.logical_not(whole)))(merged(start, BLOCK, 2 * BLOCK))
 
 
 VMEM = pl.BlockSpec(memory_space=pltpu.VMEM)
@@ -165,21 +178,21 @@
     tokens, heads = queries.shape[0], value_up.shape[1] // VAL
     return pl.pallas_call(
         own_kernel,
-        out_shape=(jax.ShapeDtypeStruct((tokens, heads * VAL), F32), jax.ShapeDtypeStruct((tokens, 128), F32)),
+        out_shape=(jax.ShapeDtypeStruct((tokens, heads * VAL), F32),) * 3,
         in_specs=[SMEM] + [VMEM] * 8,
-        out_specs=(VMEM, VMEM),
+        out_specs=(VMEM,) * 3,
         scratch_shapes=scratch_of(tokens, heads, value_up.shape[0]),
-        compiler_params=pltpu.CompilerParams(vmem_limit_bytes=40 << 20),
+        compiler_params=pltpu.CompilerParams(vmem_limit_bytes=20 << 20),
         cost_estimate=pl.CostEstimate(flops=3 << 30, bytes_accessed=8 << 20, transcendentals=1 << 21),
         name="own_part",
     )(ids, queries, *pieces, rope, key_up_t, value_up)
 
 
-def prior_part(ids, queries, near, far, w_near, w_more, w_far, key_up_t, value_up, acc, stat):
+def prior_part(ids, queries, near, far, w_near, w_more, w_far, key_up_t, value_up, state):
     tokens, heads = queries.shape[0], value_up.shape[1] // VAL
 
-    def kernel(ids, queries, near, far, w_near, wa, wb, wc, wd, we, *rest):
-        prior_kernel(ids, queries, near, far, w_near, (wa, wb), (wc, wd, we), *rest)
+    def kernel(ids, queries, near, far, w_near, wa, wb, wc, wd, *rest):
+        prior_kernel(ids, queries, near, far, w_near, (wa,), (wb, wc, wd), *rest)
 
     return pl.pallas_call(
         kernel,
@@ -187,10 +200,45 @@
         in_specs=[SMEM] + [VMEM] * 13,
         out_specs=VMEM,
         scratch_shapes=scratch_of(tokens, heads, value_up.shape[0]) + [pltpu.VMEM((ROPE + ID_ROWS, tokens), BF16)],
-        compiler_params=pltpu.CompilerParams(vmem_limit_bytes=40 << 20),
+        compiler_params=pltpu.CompilerParams(vmem_limit_bytes=20 << 20),
         cost_estimate=pl.CostEstimate(flops=4 << 30, bytes_accessed=8 << 20, transcendentals=1 << 21),
         name="prior_part",
-    )(ids, queries, near, far, w_near, *w_more, *w_far, key_up_t, value_up, acc, stat)
+    )(ids, queries, near, far, w_near, *w_more, *w_far, key_up_t, value_up, *state)
+
+
+def leaving_kernel(ids, mine, rope, out):
+    first = SHARD + ROPE
+    out[:SHARD, :] = mine[...]
+    out[SHARD:first, :] = rope[...]
+    slot = lax.broadcasted_iota(jnp.int32, (ID_ROWS, out.shape[1]), 1) // BLOCK
+    out[first:, :] = jnp.where(slot == 0, ids[0], ids[1]).astype(F32).astype(BF16)
+
+
+def leaving_part(ids, mine, rope):
+    return pl.pallas_call(
+        leaving_kernel,
+        out_shape=jax.ShapeDtypeStruct((SHARD + ROPE + ID_ROWS, mine.shape[1]), BF16),
+        in_specs=[SMEM, VMEM, VMEM],
+        out_specs=VMEM,
+        compiler_params=pltpu.CompilerParams(vmem_limit_bytes=4 << 20),
+        name="leaving_part",
+    )(ids, mine, rope)
+
+
+def weights_kernel(key_up, value_up, key_out, value_out):
+    key_out[...] = key_up[...].T
+    value_out[...] = value_up[...]
+
+
+def weights_part(key_up, value_up):
+    return pl.pallas_call(
+        weights_kernel,
+        out_shape=(jax.ShapeDtypeStruct(key_up.shape[::-1], BF16), jax.ShapeDtypeStruct(value_up.shape, BF16)),
+        in_specs=[VMEM, VMEM],
+        out_specs=(VMEM, VMEM),
+        compiler_params=pltpu.CompilerParams(vmem_limit_bytes=16 << 20),
+        name="weights_part",
+    )(key_up, value_up)
 
 
 def swapped(shard, by):
@@ -218,19 +266,18 @@
         return lax.ppermute(shard, both, [(t * peers + (h ^ by), t * peers + h) for t in range(0, groups, turn) for h in range(peers)])
 
     mine, rope = latent.T, key_rope.T
-    id_row = jnp.repeat(block_ids.astype(BF16), tokens // 2)
-    tail = joined(rope, jnp.broadcast_to(id_row[None], (ID_ROWS, tokens)))
-    by4, by2 = swapped(mine, 4), swapped(mine, 2)
-    w_near = across(joined(mine, tail), 7)
-    w_more = (across(mine, 3), across(mine, 5))
-    held = joined(mine, by4, by2)
-    got = (swapped(held, 1), swapped(by4, 2), swapped(by4, 3))
-    near = beside(joined(held, tail))
-    w_far = (swapped_there(joined(w_near[:SHARD], *w_more), 1), swapped_there(w_more[0], 2), swapped_there(w_more[0], 3))
+    by4 = swapped(mine, 4)
+    leaving = leaving_part(block_ids, mine, rope)
+    w_near, w_more = across(leaving, 7), (across(leaving, 3)[:SHARD],)
+    key_up_t, value_up = weights_part(key_up, value_up)
+    held = joined(leaving[:SHARD], by4)
+    got = tuple(swapped(held, by) for by in (1, 2, 3))
+    near = beside(joined(held, leaving[SHARD:]))
+    w_held = joined(w_near[:SHARD], *w_more)
+    w_far = tuple(swapped_there(w_held, by) for by in (1, 2, 3))
     far = beside(joined(*got))
-    key_up_t = key_up.T
-    acc, stat = own_part(block_ids, queries, (held, *got), rope, key_up_t, value_up)
-    return prior_part(block_ids, queries, near, far, w_near, w_more, w_far, key_up_t, value_up, acc, stat)
+    state = own_part(block_ids, queries, (held, *got), rope, key_up_t, value_up)
+    return prior_part(block_ids, queries, near, far, w_near, w_more, w_far, key_up_t, value_up, state)
 
 
 def solution(mesh):

time: 69.4 us -> 60.7 us (0.87)
  the two profiles are of different devices: /device:TPU:32 before, /device:TPU:64 now
where the time goes in v2:
time: 60.7 us; the launch traced here: 60.1 us
  starting transfers between devices  33.5 us (55%)
  waiting for transfers between devices  11.3 us (19%)
  Pallas kernels  10.1 us (17%)
  local copies, waits for them, and re-layouts  4.82 us (8%)
    ppermute x4, starting transfers between devices, swapped(): lax.ppermute(shard, 'head', [(i, i ^ by) for i in range(lax.axis_size('he...  19.1 us
    ppermute x2, waiting for transfers between devices, across(): lax.ppermute(shard, both, [(s * peers + (h ^ by), t * peers + h) for s, t...  11.1 us
    ppermute x3, starting transfers between devices, swapped_there(): lax.ppermute(shard, both, [(t * peers + (h ^ by), t * peers + h) for t in...  9.21 us
    pallas_call x1, Pallas kernels, prior_part(): pl.pallas_call(kernel, out_shape=jax.ShapeDtypeStruct((tokens, heads * VA...  5.29 us
    unnamed x16, local copies, waits for them, and re-layouts  4.8 us
    pallas_call x1, Pallas kernels, own_part(): pl.pallas_call(own_kernel, out_shape=(jax.ShapeDtypeStruct((tokens, heads...  3.94 us
    ppermute x2, starting transfers between devices, beside(): lax.ppermute(shard, 'seq', [(i, i + 1) for i in range(groups) if (i + 1)...  2.61 us
    ppermute x2, starting transfers between devices, across(): lax.ppermute(shard, both, [(s * peers + (h ^ by), t * peers + h) for s, t...  2.58 us
  transfers between devices with their start and end apart: 11, of which 3 were waited for; matrix products, arithmetic and copies ran while one was open for 0% of the time, Pallas kernels for 8%

profile of v2, /device:TPU:64, one launch (start us, length us, event | category | flops | bytes accessed | tf_op | source)
XLA Modules:
  0.0 60.1 jit_solution(4006178169288585599)
XLA Ops:
  0.0 9.1 %collective-permute-start = (bf16[64,512]{1,0:T(8,128)(2,1)}, bf16[64,512]{1,0:T(8,128)(2,1)S(1)}, u32[]{:S(2)}, u32[]{:S(2)}) collective-permute-start(bf16[64,512]{1,0:T(8,128)(2,1)} %bitcast.2), channel_id=1, source_target_pairs={{0,4},{1,5},{2,6},{3,7},{4,0},{5,1},{6,2},{7,3},{8,12},{9,13},{10,... | collective-permute-start | bytes 196616 | tf_op jit(solution)/shard_map/ppermute | solution.py:245
  9.1 0.8 %copy-done.2 = bf16[512,64]{0,1:T(8,128)(2,1)S(1)} copy-done((bf16[512,64]{0,1:T(8,128)(2,1)S(1)}, bf16[512,64]{0,1:T(8,128)(2,1)}, u32[]{:S(2)}) %copy-start.2) | copy-done | bytes 65560
  9.9 0.8 %copy-done.3 = bf16[512,64]{0,1:T(8,128)(2,1)S(1)} copy-done((bf16[512,64]{0,1:T(8,128)(2,1)S(1)}, bf16[512,64]{0,1:T(8,128)(2,1)}, u32[]{:S(2)}) %copy-start.3) | copy-done | bytes 65560
  10.8 0.7 %copy-done.5 = s32[2]{0:T(128)S(1)} copy-done((s32[2]{0:T(128)S(1)}, s32[2]{0:T(128)}, u32[]{:S(2)}) %copy-start.5) | copy-done | bytes 32
  11.4 0.6 leaving_part.1
  12.0 1.3 %collective-permute-start.7 = (bf16[144,512]{1,0:T(8,128)(2,1)S(1)}, bf16[144,512]{1,0:T(8,128)(2,1)S(1)}, u32[]{:S(2)}, u32[]{:S(2)}) collective-permute-start(bf16[144,512]{1,0:T(8,128)(2,1)S(1)} %leaving_part.1), channel_id=1, source_target_pairs={{251,256},{250,257},{249,258},{248,259},{255,260},{254,261},{253,2... | collective-permute-start | bytes 442376 | tf_op jit(solution)/shard_map/ppermute | solution.py:263
  13.3 1.3 %collective-permute-start.6 = (bf16[144,512]{1,0:T(8,128)(2,1)S(1)}, bf16[144,512]{1,0:T(8,128)(2,1)S(1)}, u32[]{:S(2)}, u32[]{:S(2)}) collective-permute-start(bf16[144,512]{1,0:T(8,128)(2,1)S(1)} %leaving_part.1), channel_id=1, source_target_pairs={{255,256},{254,257},{253,258},{252,259},{251,260},{250,261},{249,2... | collective-permute-start | bytes 442376 | tf_op jit(solution)/shard_map/ppermute | solution.py:263
  14.6 0.0 copy-start.4
  14.6 0.0 copy-start.6
  14.7 2.0 %collective-permute-start.4 = (bf16[128,512]{1,0:T(8,128)(2,1)S(1)}, bf16[128,512]{1,0:T(8,128)(2,1)S(1)}, u32[]{:S(2)}, u32[]{:S(2)}) collective-permute-start(bf16[128,512]{1,0:T(8,128)(2,1)S(1)} %pad_maximum_fusion.2.a), channel_id=1, source_target_pairs={{0,3},{1,2},{2,1},{3,0},{4,7},{5,6},{6,5},{7,4},{8,11},{9,10},{10,... | collective-permute-start | bytes 393224 | tf_op jit(solution)/shard_map/ppermute | solution.py:245
  16.7 6.1 %collective-permute-start.3 = (bf16[128,512]{1,0:T(8,128)(2,1)S(1)}, bf16[128,512]{1,0:T(8,128)(2,1)S(1)}, u32[]{:S(2)}, u32[]{:S(2)}) collective-permute-start(bf16[128,512]{1,0:T(8,128)(2,1)S(1)} %pad_maximum_fusion.2.a), channel_id=1, source_target_pairs={{0,2},{1,3},{2,0},{3,1},{4,6},{5,7},{6,4},{7,5},{8,10},{9,11},{10,... | collective-permute-start | bytes 393224 | tf_op jit(solution)/shard_map/ppermute | solution.py:245
  22.8 1.9 %collective-permute-start.2 = (bf16[128,512]{1,0:T(8,128)(2,1)S(1)}, bf16[128,512]{1,0:T(8,128)(2,1)S(1)}, u32[]{:S(2)}, u32[]{:S(2)}) collective-permute-start(bf16[128,512]{1,0:T(8,128)(2,1)S(1)} %pad_maximum_fusion.2.a), channel_id=1, source_target_pairs={{0,1},{1,0},{2,3},{3,2},{4,5},{5,4},{6,7},{7,6},{8,9},{9,8},{10,11... | collective-permute-start | bytes 393224 | tf_op jit(solution)/shard_map/ppermute | solution.py:245
  24.7 0.0 copy-start
  24.7 1.2 %copy-done = bf16[512,1024]{1,0:T(8,128)(2,1)S(1)} copy-done((bf16[512,1024]{1,0:T(8,128)(2,1)S(1)}, bf16[512,1024]{1,0:T(8,128)(2,1)}, u32[]{:S(2)}) %copy-start) | copy-done | bytes 1048600
  26.0 1.2 %copy-done.1 = bf16[512,1024]{1,0:T(8,128)(2,1)S(1)} copy-done((bf16[512,1024]{1,0:T(8,128)(2,1)S(1)}, bf16[512,1024]{1,0:T(8,128)(2,1)}, u32[]{:S(2)}) %copy-start.1) | copy-done | bytes 1048600
  27.2 0.4 weights_part.1
  27.6 9.9 %collective-permute-done.7 = bf16[144,512]{1,0:T(8,128)(2,1)S(1)} collective-permute-done((bf16[144,512]{1,0:T(8,128)(2,1)S(1)}, bf16[144,512]{1,0:T(8,128)(2,1)S(1)}, u32[]{:S(2)}, u32[]{:S(2)}) %collective-permute-start.7) | collective-permute-done | bytes 147488 | tf_op jit(solution)/shard_map/ppermute | solution.py:263
  37.5 1.3 %collective-permute-start.1 = (bf16[208,512]{1,0:T(8,128)(2,1)S(1)}, bf16[208,512]{1,0:T(8,128)(2,1)S(1)}, u32[]{:S(2)}, u32[]{:S(2)}) collective-permute-start(bf16[208,512]{1,0:T(8,128)(2,1)S(1)} %pad_maximum_fusion.1), channel_id=1, source_target_pairs={{0,8},{8,16},{16,24},{24,32},{32,40},{40,48},{48,56},{56,64},{64,7... | collective-permute-start | bytes 638984 | tf_op jit(solution)/shard_map/ppermute | solution.py:259
  38.8 1.2 %collective-permute-done.6.w_near = bf16[144,512]{1,0:T(8,128)(2,1)S(1)} collective-permute-done((bf16[144,512]{1,0:T(8,128)(2,1)S(1)}, bf16[144,512]{1,0:T(8,128)(2,1)S(1)}, u32[]{:S(2)}, u32[]{:S(2)}) %collective-permute-start.6) | collective-permute-done | bytes 147488 | tf_op jit(solution)/shard_map/ppermute | solution.py:263
  40.0 0.0 collective-permute-done.4.d
  40.0 0.0 collective-permute-done.3.c
  40.0 0.0 collective-permute-done.2.b
  40.1 1.3 %collective-permute-start.5 = (bf16[384,512]{1,0:T(8,128)(2,1)S(1)}, bf16[384,512]{1,0:T(8,128)(2,1)S(1)}, u32[]{:S(2)}, u32[]{:S(2)}) collective-permute-start(bf16[384,512]{1,0:T(8,128)(2,1)S(1)} %pad_maximum_fusion), channel_id=1, source_target_pairs={{0,8},{8,16},{16,24},{24,32},{32,40},{40,48},{48,56},{56,64},{64,7... | collective-permute-start | bytes 1179656 | tf_op jit(solution)/shard_map/ppermute | solution.py:259
  41.4 1.9 %collective-permute-start.10 = (bf16[128,512]{1,0:T(8,128)(2,1)S(1)}, bf16[128,512]{1,0:T(8,128)(2,1)S(1)}, u32[]{:S(2)}, u32[]{:S(2)}) collective-permute-start(bf16[128,512]{1,0:T(8,128)(2,1)S(1)} %pad_maximum_fusion.3), channel_id=1, source_target_pairs={{3,0},{2,1},{1,2},{0,3},{7,4},{6,5},{5,6},{4,7},{259,256},{258,257... | collective-permute-start | bytes 393224 | tf_op jit(solution)/shard_map/ppermute | solution.py:266
  43.3 4.6 %collective-permute-start.9 = (bf16[128,512]{1,0:T(8,128)(2,1)S(1)}, bf16[128,512]{1,0:T(8,128)(2,1)S(1)}, u32[]{:S(2)}, u32[]{:S(2)}) collective-permute-start(bf16[128,512]{1,0:T(8,128)(2,1)S(1)} %pad_maximum_fusion.3), channel_id=1, source_target_pairs={{2,0},{3,1},{0,2},{1,3},{6,4},{7,5},{4,6},{5,7},{258,256},{259,257... | collective-permute-start | bytes 393224 | tf_op jit(solution)/shard_map/ppermute | solution.py:266
  48.0 2.7 %collective-permute-start.8 = (bf16[128,512]{1,0:T(8,128)(2,1)S(1)}, bf16[128,512]{1,0:T(8,128)(2,1)S(1)}, u32[]{:S(2)}, u32[]{:S(2)}) collective-permute-start(bf16[128,512]{1,0:T(8,128)(2,1)S(1)} %pad_maximum_fusion.3), channel_id=1, source_target_pairs={{1,0},{0,1},{3,2},{2,3},{5,4},{4,5},{7,6},{6,7},{257,256},{256,257... | collective-permute-start | bytes 393224 | tf_op jit(solution)/shard_map/ppermute | solution.py:266
  50.7 3.9 %own_part.1 = (f32[512,1024]{1,0:T(8,128)S(1)}, f32[512,1024]{1,0:T(8,128)S(1)}, f32[512,1024]{1,0:T(8,128)S(1)}) custom-call(s32[2]{0:T(128)S(1)} %copy-done.6, bf16[512,1536]{1,0:T(8,128)(2,1)S(1)} %copy-done.7, bf16[128,512]{1,0:T(8,128)(2,1)S(1)} %pad_maximum_fusion.2.a, bf16[128,512]{1,0:T(8,128)(2,1)S(1)} %collective-permute-done.2.b, ...), custom_call_target="tpu_custom_call" | custom-call | flops 3221225472 | bytes 8388608 | tf_op jit(solution)/shard_map/own_part/pallas_call | solution.py:179
  54.6 0.0 collective-permute-done.10.wd
  54.6 0.0 collective-permute-done.9.wc
  54.6 0.2 collective-permute-done.8.wb
  54.8 0.0 collective-permute-done.5.far
  54.8 5.3 %prior_part.1 = bf16[512,1024]{1,0:T(8,128)(2,1)} custom-call(s32[2]{0:T(128)S(1)} %copy-done.6, bf16[512,1536]{1,0:T(8,128)(2,1)S(1)} %copy-done.7, bf16[208,512]{1,0:T(8,128)(2,1)S(1)} %collective-permute-done.1.near, bf16[384,512]{1,0:T(8,128)(2,1)S(1)} %collective-permute-done.5.far, bf16[144,512]{1,0:T(8,128)(2,1)S(1)} %collective-permute-done.6.w_near, ...), custom_call_target="tpu_custom_call" | custom-call | flops 4294967296 | bytes 8388608 | tf_op jit(solution)/shard_map/prior_part/pallas_call | solution.py:197
  (18 shorter events, 0.1 us)
Async XLA Ops:
  0.0 14.6 %collective-permute-start = (bf16[64,512]{1,0:T(8,128)(2,1)}, bf16[64,512]{1,0:T(8,128)(2,1)S(1)}, u32[]{:S(2)}, u32[]{:S(2)}) collective-permute-start(bf16[64,512]{1,0:T(8,128)(2,1)} %bitcast.2), channel_id=1, source_target_pairs={{0,4},{1,5},{2,6},{3,7},{4,0},{5,1},{6,2},{7,3},{8,12},{9,13},{10,... | collective-permute-start | bytes 196616 | tf_op jit(solution)/shard_map/ppermute | solution.py:245
  9.1 0.9 %copy-start.2 = (bf16[512,64]{0,1:T(8,128)(2,1)S(1)}, bf16[512,64]{0,1:T(8,128)(2,1)}, u32[]{:S(2)}) copy-start(bf16[512,64]{0,1:T(8,128)(2,1)} %param.7) | copy-start | bytes 196612
  9.9 0.8 %copy-start.3 = (bf16[512,64]{0,1:T(8,128)(2,1)S(1)}, bf16[512,64]{0,1:T(8,128)(2,1)}, u32[]{:S(2)}) copy-start(bf16[512,64]{0,1:T(8,128)(2,1)} %param.8) | copy-start | bytes 196612
  10.8 0.7 %copy-start.5 = (s32[2]{0:T(128)S(1)}, s32[2]{0:T(128)}, u32[]{:S(2)}) copy-start(s32[2]{0:T(128)} %ids.5) | copy-start | bytes 28
  12.0 25.5 %collective-permute-start.7 = (bf16[144,512]{1,0:T(8,128)(2,1)S(1)}, bf16[144,512]{1,0:T(8,128)(2,1)S(1)}, u32[]{:S(2)}, u32[]{:S(2)}) collective-permute-start(bf16[144,512]{1,0:T(8,128)(2,1)S(1)} %leaving_part.1), channel_id=1, source_target_pairs={{251,256},{250,257},{249,258},{248,259},{255,260},{254,261},{253,2... | collective-permute-start | bytes 442376 | tf_op jit(solution)/shard_map/ppermute | solution.py:263
  13.3 26.7 %collective-permute-start.6 = (bf16[144,512]{1,0:T(8,128)(2,1)S(1)}, bf16[144,512]{1,0:T(8,128)(2,1)S(1)}, u32[]{:S(2)}, u32[]{:S(2)}) collective-permute-start(bf16[144,512]{1,0:T(8,128)(2,1)S(1)} %leaving_part.1), channel_id=1, source_target_pairs={{255,256},{254,257},{253,258},{252,259},{251,260},{250,261},{249,2... | collective-permute-start | bytes 442376 | tf_op jit(solution)/shard_map/ppermute | solution.py:263
  14.6 36.0 %copy-start.4 = (bf16[512,64]{0,1:T(8,128)(2,1)S(1)}, bf16[512,64]{0,1:T(8,128)(2,1)}, u32[]{:S(2)}) copy-start(bf16[512,64]{0,1:T(8,128)(2,1)} %param.8) | copy-start | bytes 196612
  14.6 36.0 %copy-start.6 = (s32[2]{0:T(128)S(1)}, s32[2]{0:T(128)}, u32[]{:S(2)}) copy-start(s32[2]{0:T(128)} %ids.5) | copy-start | bytes 28
  14.7 25.3 %collective-permute-start.4 = (bf16[128,512]{1,0:T(8,128)(2,1)S(1)}, bf16[128,512]{1,0:T(8,128)(2,1)S(1)}, u32[]{:S(2)}, u32[]{:S(2)}) collective-permute-start(bf16[128,512]{1,0:T(8,128)(2,1)S(1)} %pad_maximum_fusion.2.a), channel_id=1, source_target_pairs={{0,3},{1,2},{2,1},{3,0},{4,7},{5,6},{6,5},{7,4},{8,11},{9,10},{10,... | collective-permute-start | bytes 393224 | tf_op jit(solution)/shard_map/ppermute | solution.py:245
  16.7 23.3 %collective-permute-start.3 = (bf16[128,512]{1,0:T(8,128)(2,1)S(1)}, bf16[128,512]{1,0:T(8,128)(2,1)S(1)}, u32[]{:S(2)}, u32[]{:S(2)}) collective-permute-start(bf16[128,512]{1,0:T(8,128)(2,1)S(1)} %pad_maximum_fusion.2.a), channel_id=1, source_target_pairs={{0,2},{1,3},{2,0},{3,1},{4,6},{5,7},{6,4},{7,5},{8,10},{9,11},{10,... | collective-permute-start | bytes 393224 | tf_op jit(solution)/shard_map/ppermute | solution.py:245
  22.8 17.2 %collective-permute-start.2 = (bf16[128,512]{1,0:T(8,128)(2,1)S(1)}, bf16[128,512]{1,0:T(8,128)(2,1)S(1)}, u32[]{:S(2)}, u32[]{:S(2)}) collective-permute-start(bf16[128,512]{1,0:T(8,128)(2,1)S(1)} %pad_maximum_fusion.2.a), channel_id=1, source_target_pairs={{0,1},{1,0},{2,3},{3,2},{4,5},{5,4},{6,7},{7,6},{8,9},{9,8},{10,11... | collective-permute-start | bytes 393224 | tf_op jit(solution)/shard_map/ppermute | solution.py:245
  24.7 1.2 %copy-start = (bf16[512,1024]{1,0:T(8,128)(2,1)S(1)}, bf16[512,1024]{1,0:T(8,128)(2,1)}, u32[]{:S(2)}) copy-start(bf16[512,1024]{1,0:T(8,128)(2,1)} %key_up.1) | copy-start | bytes 3145732
  25.9 1.2 %copy-start.1 = (bf16[512,1024]{1,0:T(8,128)(2,1)S(1)}, bf16[512,1024]{1,0:T(8,128)(2,1)}, u32[]{:S(2)}) copy-start(bf16[512,1024]{1,0:T(8,128)(2,1)} %value_up.1) | copy-start | bytes 3145732
  27.2 23.5 %copy-start.7 = (bf16[512,1536]{1,0:T(8,128)(2,1)S(1)}, bf16[512,1536]{1,0:T(8,128)(2,1)}, u32[]{:S(2)}) copy-start(bf16[512,1536]{1,0:T(8,128)(2,1)} %queries.3) | copy-start | bytes 4718596
  37.5 17.3 %collective-permute-start.1 = (bf16[208,512]{1,0:T(8,128)(2,1)S(1)}, bf16[208,512]{1,0:T(8,128)(2,1)S(1)}, u32[]{:S(2)}, u32[]{:S(2)}) collective-permute-start(bf16[208,512]{1,0:T(8,128)(2,1)S(1)} %pad_maximum_fusion.1), channel_id=1, source_target_pairs={{0,8},{8,16},{16,24},{24,32},{32,40},{40,48},{48,56},{56,64},{64,7... | collective-permute-start | bytes 638984 | tf_op jit(solution)/shard_map/ppermute | solution.py:259
  40.1 14.8 %collective-permute-start.5 = (bf16[384,512]{1,0:T(8,128)(2,1)S(1)}, bf16[384,512]{1,0:T(8,128)(2,1)S(1)}, u32[]{:S(2)}, u32[]{:S(2)}) collective-permute-start(bf16[384,512]{1,0:T(8,128)(2,1)S(1)} %pad_maximum_fusion), channel_id=1, source_target_pairs={{0,8},{8,16},{16,24},{24,32},{32,40},{40,48},{48,56},{56,64},{64,7... | collective-permute-start | bytes 1179656 | tf_op jit(solution)/shard_map/ppermute | solution.py:259
  41.4 13.2 %collective-permute-start.10 = (bf16[128,512]{1,0:T(8,128)(2,1)S(1)}, bf16[128,512]{1,0:T(8,128)(2,1)S(1)}, u32[]{:S(2)}, u32[]{:S(2)}) collective-permute-start(bf16[128,512]{1,0:T(8,128)(2,1)S(1)} %pad_maximum_fusion.3), channel_id=1, source_target_pairs={{3,0},{2,1},{1,2},{0,3},{7,4},{6,5},{5,6},{4,7},{259,256},{258,257... | collective-permute-start | bytes 393224 | tf_op jit(solution)/shard_map/ppermute | solution.py:266
  43.3 11.3 %collective-permute-start.9 = (bf16[128,512]{1,0:T(8,128)(2,1)S(1)}, bf16[128,512]{1,0:T(8,128)(2,1)S(1)}, u32[]{:S(2)}, u32[]{:S(2)}) collective-permute-start(bf16[128,512]{1,0:T(8,128)(2,1)S(1)} %pad_maximum_fusion.3), channel_id=1, source_target_pairs={{2,0},{3,1},{0,2},{1,3},{6,4},{7,5},{4,6},{5,7},{258,256},{259,257... | collective-permute-start | bytes 393224 | tf_op jit(solution)/shard_map/ppermute | solution.py:266
  48.0 6.9 %collective-permute-start.8 = (bf16[128,512]{1,0:T(8,128)(2,1)S(1)}, bf16[128,512]{1,0:T(8,128)(2,1)S(1)}, u32[]{:S(2)}, u32[]{:S(2)}) collective-permute-start(bf16[128,512]{1,0:T(8,128)(2,1)S(1)} %pad_maximum_fusion.3), channel_id=1, source_target_pairs={{1,0},{0,1},{3,2},{2,3},{5,4},{4,5},{7,6},{6,7},{257,256},{256,257... | collective-permute-start | bytes 393224 | tf_op jit(solution)/shard_map/ppermute | solution.py:266

commit v3 on v2

--- a/solution.py
+++ b/solution.py
@@ -95,28 +95,24 @@
             top_out[pl.ds(at, BLOCK), columns] = jnp.broadcast_to(top, (BLOCK, VAL))
 
 
-def prior_kernel(ids, queries, near, far, w_near, w_more, w_far, key_up_t, value_up, acc_in, sum_in, top_in, out, lat, keys, values, tail):
+def prior_kernel(ids, queries, near, far, there, across, key_up_t, value_up, acc_in, sum_in, top_in, out, lat, keys, values, tail):
     turn = lax.axis_size("seq") // 2
     crossing = lax.rem(lax.axis_index("seq"), turn) == 0
     spot = lax.axis_index("head")
 
-    def positions():
-        one = jnp.max(tail[ROPE : ROPE + 1, :128].astype(F32)).astype(jnp.int32)
-        two = jnp.max(tail[ROPE : ROPE + 1, BLOCK : BLOCK + 128].astype(F32)).astype(jnp.int32)
-        return one, two
-
-    def from_chip_beside():
-        tail[...] = near[NEAR * SHARD :, :]
-
-    def from_other_half():
-        tail[...] = w_near[SHARD:, :]
-
-    pl.when(crossing)(from_other_half)
-    pl.when(jnp.logical_not(crossing))(from_chip_beside)
-    one, two = positions()
+    def tail_from(source):
+        def body():
+            tail[...] = source[...]
+
+        return body
+
+    pl.when(crossing)(tail_from(there.at[SHARD:]))
+    pl.when(jnp.logical_not(crossing))(tail_from(near.at[NEAR * SHARD :]))
+    one = jnp.max(tail[ROPE : ROPE + 1, :128].astype(F32)).astype(jnp.int32)
+    two = jnp.max(tail[ROPE : ROPE + 1, BLOCK : BLOCK + 128].astype(F32)).astype(jnp.int32)
     first = pl.multiple_of(jnp.where(one < two, 0, BLOCK), BLOCK)
     low, high = jnp.minimum(one, two), jnp.maximum(one, two)
-    pl.when(crossing)(lambda: place((w_near.at[:SHARD], *w_more, *w_far), spot ^ 7, first, lat))
+    pl.when(crossing)(lambda: place(across, spot ^ 4, first, lat))
     pl.when(jnp.logical_not(crossing))(lambda: place((near.at[: NEAR * SHARD], far), spot, first, lat))
     place_rope(tail.at[:ROPE], first, keys)
     project(lat, key_up_t, value_up, keys, values)
@@ -188,11 +184,11 @@
     )(ids, queries, *pieces, rope, key_up_t, value_up)
 
 
-def prior_part(ids, queries, near, far, w_near, w_more, w_far, key_up_t, value_up, state):
+def prior_part(ids, queries, near, far, there, across, key_up_t, value_up, state):
     tokens, heads = queries.shape[0], value_up.shape[1] // VAL
 
-    def kernel(ids, queries, near, far, w_near, wa, wb, wc, wd, *rest):
-        prior_kernel(ids, queries, near, far, w_near, (wa,), (wb, wc, wd), *rest)
+    def kernel(ids, queries, near, far, there, wa, wb, wc, wd, *rest):
+        prior_kernel(ids, queries, near, far, there, (wa, wb, wc, wd), *rest)
 
     return pl.pallas_call(
         kernel,
@@ -203,7 +199,7 @@
         compiler_params=pltpu.CompilerParams(vmem_limit_bytes=20 << 20),
         cost_estimate=pl.CostEstimate(flops=4 << 30, bytes_accessed=8 << 20, transcendentals=1 << 21),
         name="prior_part",
-    )(ids, queries, near, far, w_near, *w_more, *w_far, key_up_t, value_up, *state)
+    )(ids, queries, near, far, there, *across, key_up_t, value_up, *state)
 
 
 def leaving_kernel(ids, mine, rope, out):
@@ -255,29 +251,30 @@
     both = ("seq", "head")
     tokens = queries.shape[0]
 
-    def beside(shard):
-        return lax.ppermute(shard, "seq", [(i, i + 1) for i in range(groups) if (i + 1) % turn])
-
-    def across(shard, by):
-        pairs = [(i, (i + 1) % groups) for i in range(turn - 1, groups, turn)]
-        return lax.ppermute(shard, both, [(s * peers + (h ^ by), t * peers + h) for s, t in pairs for h in range(peers)])
-
-    def swapped_there(shard, by):
-        return lax.ppermute(shard, both, [(t * peers + (h ^ by), t * peers + h) for t in range(0, groups, turn) for h in range(peers)])
+    steps = [(i, (i + 1) % groups) for i in range(groups)]
+    beside = [(s, t) for s, t in steps if t % turn]
+    crossing = [(s, t) for s, t in steps if t % turn == 0]
+    within = [(t, t) for _, t in crossing]
+
+    def onward(shard, pairs, by=0):
+        sent = [(s * peers + (h ^ by), t * peers + h) for s, t in pairs for h in range(peers)]
+        return lax.ppermute(shard, both, sent)
 
     mine, rope = latent.T, key_rope.T
     by4 = swapped(mine, 4)
+    arrived = onward(mine, crossing, 4)
     leaving = leaving_part(block_ids, mine, rope)
-    w_near, w_more = across(leaving, 7), (across(leaving, 3)[:SHARD],)
-    key_up_t, value_up = weights_part(key_up, value_up)
+    there = onward(leaving, crossing, 4)
     held = joined(leaving[:SHARD], by4)
     got = tuple(swapped(held, by) for by in (1, 2, 3))
-    near = beside(joined(held, leaving[SHARD:]))
-    w_held = joined(w_near[:SHARD], *w_more)
-    w_far = tuple(swapped_there(w_held, by) for by in (1, 2, 3))
-    far = beside(joined(*got))
+    arrived, key_up, value_up = lax.optimization_barrier((arrived, key_up, value_up))
+    key_up_t, value_up = weights_part(key_up, value_up)
+    w_held = joined(arrived, onward(arrived, within, 4))
+    near = onward(joined(held, leaving[SHARD:]), beside)
+    far = onward(joined(*got), beside)
     state = own_part(block_ids, queries, (held, *got), rope, key_up_t, value_up)
-    return prior_part(block_ids, queries, near, far, w_near, w_more, w_far, key_up_t, value_up, state)
+    across = (w_held, *(onward(w_held, within, by) for by in (1, 2, 3)))
+    return prior_part(block_ids, queries, near, far, there, across, key_up_t, value_up, state)
 
 
 def solution(mesh):

time: 60.7 us -> 58.7 us (0.967)
  waiting for transfers between devices: 11.3 us -> 0.94 us
  starting transfers between devices: 33.5 us -> 41.7 us
    ppermute x7 -> x8, waiting for transfers between devices: 11.3 us -> 0.93 us  [onward(): return lax.ppermute(shard, both, sent)]
    ppermute x7 -> x8, starting transfers between devices: 14.4 us -> 22.6 us  [onward(): return lax.ppermute(shard, both, sent)]
    unnamed x16 -> x17, local copies, waits for them, and re-layouts: 4.8 us -> 4.79 us
  transfers between devices with their start and end apart: 11 -> 12, of which waited for: 3 -> 1; matrix products, arithmetic and copies ran while one was open for 0% -> 0% of each run, Pallas kernels for 8% -> 8%
where the time goes in v3:
time: 58.7 us; the launch traced here: 58.4 us
  starting transfers between devices  41.7 us (71%)
  Pallas kernels  10.6 us (18%)
  local copies, waits for them, and re-layouts  4.81 us (8%)
  waiting for transfers between devices  0.94 us (2%)
    ppermute x8, starting transfers between devices, onward(): return lax.ppermute(shard, both, sent)  22.6 us
    ppermute x4, starting transfers between devices, swapped(): lax.ppermute(shard, 'head', [(i, i ^ by) for i in range(lax.axis_size('he...  19.1 us
    pallas_call x1, Pallas kernels, prior_part(): pl.pallas_call(kernel, out_shape=jax.ShapeDtypeStruct((tokens, heads * VA...  5.71 us
    unnamed x17, local copies, waits for them, and re-layouts  4.79 us
    pallas_call x1, Pallas kernels, own_part(): pl.pallas_call(own_kernel, out_shape=(jax.ShapeDtypeStruct((tokens, heads...  3.96 us
  transfers between devices with their start and end apart: 12, of which 1 were waited for; matrix products, arithmetic and copies ran while one was open for 0% of the time, Pallas kernels for 8%

profile of v3, /device:TPU:64, one launch (start us, length us, event | category | flops | bytes accessed | tf_op | source)
XLA Modules:
  0.0 58.4 jit_solution(954804080831308722)
XLA Ops:
  0.0 9.1 %collective-permute-start = (bf16[64,512]{1,0:T(8,128)(2,1)}, bf16[64,512]{1,0:T(8,128)(2,1)S(1)}, u32[]{:S(2)}, u32[]{:S(2)}) collective-permute-start(bf16[64,512]{1,0:T(8,128)(2,1)} %bitcast.2), channel_id=1, source_target_pairs={{0,4},{1,5},{2,6},{3,7},{4,0},{5,1},{6,2},{7,3},{8,12},{9,13},{10,... | collective-permute-start | bytes 196616 | tf_op jit(solution)/shard_map/ppermute | solution.py:241
  9.1 1.3 %collective-permute-start.7 = (bf16[64,512]{1,0:T(8,128)(2,1)}, bf16[64,512]{1,0:T(8,128)(2,1)S(1)}, u32[]{:S(2)}, u32[]{:S(2)}) collective-permute-start(bf16[64,512]{1,0:T(8,128)(2,1)} %bitcast.3), channel_id=1, source_target_pairs={{252,256},{253,257},{254,258},{255,259},{248,260},{249,261},{250,2... | collective-permute-start | bytes 196616 | tf_op jit(solution)/shard_map/ppermute | solution.py:261
  10.4 0.8 %copy-done.2 = bf16[512,64]{0,1:T(8,128)(2,1)S(1)} copy-done((bf16[512,64]{0,1:T(8,128)(2,1)S(1)}, bf16[512,64]{0,1:T(8,128)(2,1)}, u32[]{:S(2)}) %copy-start.2) | copy-done | bytes 65560
  11.2 0.8 %copy-done.3 = bf16[512,64]{0,1:T(8,128)(2,1)S(1)} copy-done((bf16[512,64]{0,1:T(8,128)(2,1)S(1)}, bf16[512,64]{0,1:T(8,128)(2,1)}, u32[]{:S(2)}) %copy-start.3) | copy-done | bytes 65560
  12.1 0.7 %copy-done.5 = s32[2]{0:T(128)S(1)} copy-done((s32[2]{0:T(128)S(1)}, s32[2]{0:T(128)}, u32[]{:S(2)}) %copy-start.5) | copy-done | bytes 32
  12.7 0.6 leaving_part.1
  13.3 0.0 copy-start.4
  13.3 0.0 copy-start.6
  13.3 1.4 %collective-permute-start.6 = (bf16[144,512]{1,0:T(8,128)(2,1)S(1)}, bf16[144,512]{1,0:T(8,128)(2,1)S(1)}, u32[]{:S(2)}, u32[]{:S(2)}) collective-permute-start(bf16[144,512]{1,0:T(8,128)(2,1)S(1)} %leaving_part.1), channel_id=1, source_target_pairs={{252,256},{253,257},{254,258},{255,259},{248,260},{249,261},{250,2... | collective-permute-start | bytes 442376 | tf_op jit(solution)/shard_map/ppermute | solution.py:261
  14.8 0.0 collective-permute-done
  14.8 2.0 %collective-permute-start.4 = (bf16[128,512]{1,0:T(8,128)(2,1)S(1)}, bf16[128,512]{1,0:T(8,128)(2,1)S(1)}, u32[]{:S(2)}, u32[]{:S(2)}) collective-permute-start(bf16[128,512]{1,0:T(8,128)(2,1)S(1)} %pad_maximum_fusion.2.a), channel_id=1, source_target_pairs={{0,3},{1,2},{2,1},{3,0},{4,7},{5,6},{6,5},{7,4},{8,11},{9,10},{10,... | collective-permute-start | bytes 393224 | tf_op jit(solution)/shard_map/ppermute | solution.py:241
  16.8 6.1 %collective-permute-start.3 = (bf16[128,512]{1,0:T(8,128)(2,1)S(1)}, bf16[128,512]{1,0:T(8,128)(2,1)S(1)}, u32[]{:S(2)}, u32[]{:S(2)}) collective-permute-start(bf16[128,512]{1,0:T(8,128)(2,1)S(1)} %pad_maximum_fusion.2.a), channel_id=1, source_target_pairs={{0,2},{1,3},{2,0},{3,1},{4,6},{5,7},{6,4},{7,5},{8,10},{9,11},{10,... | collective-permute-start | bytes 393224 | tf_op jit(solution)/shard_map/ppermute | solution.py:241
  22.9 1.9 %collective-permute-start.2 = (bf16[128,512]{1,0:T(8,128)(2,1)S(1)}, bf16[128,512]{1,0:T(8,128)(2,1)S(1)}, u32[]{:S(2)}, u32[]{:S(2)}) collective-permute-start(bf16[128,512]{1,0:T(8,128)(2,1)S(1)} %pad_maximum_fusion.2.a), channel_id=1, source_target_pairs={{0,1},{1,0},{2,3},{3,2},{4,5},{5,4},{6,7},{7,6},{8,9},{9,8},{10,11... | collective-permute-start | bytes 393224 | tf_op jit(solution)/shard_map/ppermute | solution.py:241
  24.8 0.0 collective-permute-done.7
  24.9 7.0 %collective-permute-start.8 = (bf16[64,512]{1,0:T(8,128)(2,1)S(1)}, bf16[64,512]{1,0:T(8,128)(2,1)S(1)}, u32[]{:S(2)}, u32[]{:S(2)}) collective-permute-start(bf16[64,512]{1,0:T(8,128)(2,1)S(1)} %collective-permute-done.7), channel_id=1, source_target_pairs={{260,256},{261,257},{262,258},{263,259},{256,260},{257,261},{258,2... | collective-permute-start | bytes 196616 | tf_op jit(solution)/shard_map/ppermute | solution.py:261
  31.9 0.0 copy-start
  31.9 1.2 %copy-done = bf16[512,1024]{1,0:T(8,128)(2,1)S(1)} copy-done((bf16[512,1024]{1,0:T(8,128)(2,1)S(1)}, bf16[512,1024]{1,0:T(8,128)(2,1)}, u32[]{:S(2)}) %copy-start) | copy-done | bytes 1048600
  33.1 1.2 %copy-done.1 = bf16[512,1024]{1,0:T(8,128)(2,1)S(1)} copy-done((bf16[512,1024]{1,0:T(8,128)(2,1)S(1)}, bf16[512,1024]{1,0:T(8,128)(2,1)}, u32[]{:S(2)}) %copy-start.1) | copy-done | bytes 1048600
  34.3 0.4 weights_part.1
  34.7 0.0 collective-permute-done.4.d
  34.7 1.4 %collective-permute-start.1 = (bf16[208,512]{1,0:T(8,128)(2,1)S(1)}, bf16[208,512]{1,0:T(8,128)(2,1)S(1)}, u32[]{:S(2)}, u32[]{:S(2)}) collective-permute-start(bf16[208,512]{1,0:T(8,128)(2,1)S(1)} %pad_maximum_fusion.1), channel_id=1, source_target_pairs={{0,8},{1,9},{2,10},{3,11},{4,12},{5,13},{6,14},{7,15},{8,16},{9,17... | collective-permute-start | bytes 638984 | tf_op jit(solution)/shard_map/ppermute | solution.py:261
  36.2 0.0 collective-permute-done.3.c
  36.2 1.3 %collective-permute-start.5 = (bf16[384,512]{1,0:T(8,128)(2,1)S(1)}, bf16[384,512]{1,0:T(8,128)(2,1)S(1)}, u32[]{:S(2)}, u32[]{:S(2)}) collective-permute-start(bf16[384,512]{1,0:T(8,128)(2,1)S(1)} %pad_maximum_fusion), channel_id=1, source_target_pairs={{0,8},{1,9},{2,10},{3,11},{4,12},{5,13},{6,14},{7,15},{8,16},{9,17... | collective-permute-start | bytes 1179656 | tf_op jit(solution)/shard_map/ppermute | solution.py:261
  37.6 2.8 %collective-permute-start.11 = (bf16[128,512]{1,0:T(8,128)(2,1)S(1)}, bf16[128,512]{1,0:T(8,128)(2,1)S(1)}, u32[]{:S(2)}, u32[]{:S(2)}) collective-permute-start(bf16[128,512]{1,0:T(8,128)(2,1)S(1)} %constant_dynamic-update-slice_fusion.wa), channel_id=1, source_target_pairs={{259,256},{258,257},{257,258},{256,259},{263,260},{262,261},{261,2... | collective-permute-start | bytes 393224 | tf_op jit(solution)/shard_map/ppermute | solution.py:261
  40.4 5.4 %collective-permute-start.10 = (bf16[128,512]{1,0:T(8,128)(2,1)S(1)}, bf16[128,512]{1,0:T(8,128)(2,1)S(1)}, u32[]{:S(2)}, u32[]{:S(2)}) collective-permute-start(bf16[128,512]{1,0:T(8,128)(2,1)S(1)} %constant_dynamic-update-slice_fusion.wa), channel_id=1, source_target_pairs={{258,256},{259,257},{256,258},{257,259},{262,260},{263,261},{260,2... | collective-permute-start | bytes 393224 | tf_op jit(solution)/shard_map/ppermute | solution.py:261
  45.8 0.0 collective-permute-done.6.there
  45.8 1.9 %collective-permute-start.9 = (bf16[128,512]{1,0:T(8,128)(2,1)S(1)}, bf16[128,512]{1,0:T(8,128)(2,1)S(1)}, u32[]{:S(2)}, u32[]{:S(2)}) collective-permute-start(bf16[128,512]{1,0:T(8,128)(2,1)S(1)} %constant_dynamic-update-slice_fusion.wa), channel_id=1, source_target_pairs={{257,256},{256,257},{259,258},{258,259},{261,260},{260,261},{263,2... | collective-permute-start | bytes 393224 | tf_op jit(solution)/shard_map/ppermute | solution.py:261
  47.7 4.0 %own_part.1 = (f32[512,1024]{1,0:T(8,128)S(1)}, f32[512,1024]{1,0:T(8,128)S(1)}, f32[512,1024]{1,0:T(8,128)S(1)}) custom-call(s32[2]{0:T(128)S(1)} %copy-done.6, bf16[512,1536]{1,0:T(8,128)(2,1)S(1)} %copy-done.7, bf16[128,512]{1,0:T(8,128)(2,1)S(1)} %pad_maximum_fusion.2.a, bf16[128,512]{1,0:T(8,128)(2,1)S(1)} %collective-permute-done.2.b, ...), custom_call_target="tpu_custom_call" | custom-call | flops 3221225472 | bytes 8388608 | tf_op jit(solution)/shard_map/own_part/pallas_call | solution.py:175
  51.7 0.0 collective-permute-done.11.wd
  51.7 0.0 collective-permute-done.10.wc
  51.7 0.9 %collective-permute-done.9.wb = bf16[128,512]{1,0:T(8,128)(2,1)S(1)} collective-permute-done((bf16[128,512]{1,0:T(8,128)(2,1)S(1)}, bf16[128,512]{1,0:T(8,128)(2,1)S(1)}, u32[]{:S(2)}, u32[]{:S(2)}) %collective-permute-start.9) | collective-permute-done | bytes 131104 | tf_op jit(solution)/shard_map/ppermute | solution.py:261
  52.6 5.7 %prior_part.1 = bf16[512,1024]{1,0:T(8,128)(2,1)} custom-call(s32[2]{0:T(128)S(1)} %copy-done.6, bf16[512,1536]{1,0:T(8,128)(2,1)S(1)} %copy-done.7, bf16[208,512]{1,0:T(8,128)(2,1)S(1)} %collective-permute-done.1.near, bf16[384,512]{1,0:T(8,128)(2,1)S(1)} %collective-permute-done.5.far, bf16[144,512]{1,0:T(8,128)(2,1)S(1)} %collective-permute-done.6.there, ...), custom_call_target="tpu_custom_call" | custom-call | flops 4294967296 | bytes 8388608 | tf_op jit(solution)/shard_map/prior_part/pallas_call | solution.py:193
  (19 shorter events, 0.1 us)
Async XLA Ops:
  0.0 14.8 %collective-permute-start = (bf16[64,512]{1,0:T(8,128)(2,1)}, bf16[64,512]{1,0:T(8,128)(2,1)S(1)}, u32[]{:S(2)}, u32[]{:S(2)}) collective-permute-start(bf16[64,512]{1,0:T(8,128)(2,1)} %bitcast.2), channel_id=1, source_target_pairs={{0,4},{1,5},{2,6},{3,7},{4,0},{5,1},{6,2},{7,3},{8,12},{9,13},{10,... | collective-permute-start | bytes 196616 | tf_op jit(solution)/shard_map/ppermute | solution.py:241
  9.1 15.8 %collective-permute-start.7 = (bf16[64,512]{1,0:T(8,128)(2,1)}, bf16[64,512]{1,0:T(8,128)(2,1)S(1)}, u32[]{:S(2)}, u32[]{:S(2)}) collective-permute-start(bf16[64,512]{1,0:T(8,128)(2,1)} %bitcast.3), channel_id=1, source_target_pairs={{252,256},{253,257},{254,258},{255,259},{248,260},{249,261},{250,2... | collective-permute-start | bytes 196616 | tf_op jit(solution)/shard_map/ppermute | solution.py:261
  10.4 0.8 %copy-start.2 = (bf16[512,64]{0,1:T(8,128)(2,1)S(1)}, bf16[512,64]{0,1:T(8,128)(2,1)}, u32[]{:S(2)}) copy-start(bf16[512,64]{0,1:T(8,128)(2,1)} %param.7) | copy-start | bytes 196612
  11.2 0.8 %copy-start.3 = (bf16[512,64]{0,1:T(8,128)(2,1)S(1)}, bf16[512,64]{0,1:T(8,128)(2,1)}, u32[]{:S(2)}) copy-start(bf16[512,64]{0,1:T(8,128)(2,1)} %param.8) | copy-start | bytes 196612
  12.1 0.7 %copy-start.5 = (s32[2]{0:T(128)S(1)}, s32[2]{0:T(128)}, u32[]{:S(2)}) copy-start(s32[2]{0:T(128)} %ids.5) | copy-start | bytes 28
  13.3 34.4 %copy-start.4 = (bf16[512,64]{0,1:T(8,128)(2,1)S(1)}, bf16[512,64]{0,1:T(8,128)(2,1)}, u32[]{:S(2)}) copy-start(bf16[512,64]{0,1:T(8,128)(2,1)} %param.8) | copy-start | bytes 196612
  13.3 34.4 %copy-start.6 = (s32[2]{0:T(128)S(1)}, s32[2]{0:T(128)}, u32[]{:S(2)}) copy-start(s32[2]{0:T(128)} %ids.5) | copy-start | bytes 28
  13.3 32.5 %collective-permute-start.6 = (bf16[144,512]{1,0:T(8,128)(2,1)S(1)}, bf16[144,512]{1,0:T(8,128)(2,1)S(1)}, u32[]{:S(2)}, u32[]{:S(2)}) collective-permute-start(bf16[144,512]{1,0:T(8,128)(2,1)S(1)} %leaving_part.1), channel_id=1, source_target_pairs={{252,256},{253,257},{254,258},{255,259},{248,260},{249,261},{250,2... | collective-permute-start | bytes 442376 | tf_op jit(solution)/shard_map/ppermute | solution.py:261
  14.8 19.9 %collective-permute-start.4 = (bf16[128,512]{1,0:T(8,128)(2,1)S(1)}, bf16[128,512]{1,0:T(8,128)(2,1)S(1)}, u32[]{:S(2)}, u32[]{:S(2)}) collective-permute-start(bf16[128,512]{1,0:T(8,128)(2,1)S(1)} %pad_maximum_fusion.2.a), channel_id=1, source_target_pairs={{0,3},{1,2},{2,1},{3,0},{4,7},{5,6},{6,5},{7,4},{8,11},{9,10},{10,... | collective-permute-start | bytes 393224 | tf_op jit(solution)/shard_map/ppermute | solution.py:241
  16.8 19.3 %collective-permute-start.3 = (bf16[128,512]{1,0:T(8,128)(2,1)S(1)}, bf16[128,512]{1,0:T(8,128)(2,1)S(1)}, u32[]{:S(2)}, u32[]{:S(2)}) collective-permute-start(bf16[128,512]{1,0:T(8,128)(2,1)S(1)} %pad_maximum_fusion.2.a), channel_id=1, source_target_pairs={{0,2},{1,3},{2,0},{3,1},{4,6},{5,7},{6,4},{7,5},{8,10},{9,11},{10,... | collective-permute-start | bytes 393224 | tf_op jit(solution)/shard_map/ppermute | solution.py:241
  22.9 13.3 %collective-permute-start.2 = (bf16[128,512]{1,0:T(8,128)(2,1)S(1)}, bf16[128,512]{1,0:T(8,128)(2,1)S(1)}, u32[]{:S(2)}, u32[]{:S(2)}) collective-permute-start(bf16[128,512]{1,0:T(8,128)(2,1)S(1)} %pad_maximum_fusion.2.a), channel_id=1, source_target_pairs={{0,1},{1,0},{2,3},{3,2},{4,5},{5,4},{6,7},{7,6},{8,9},{9,8},{10,11... | collective-permute-start | bytes 393224 | tf_op jit(solution)/shard_map/ppermute | solution.py:241
  24.9 12.7 %collective-permute-start.8 = (bf16[64,512]{1,0:T(8,128)(2,1)S(1)}, bf16[64,512]{1,0:T(8,128)(2,1)S(1)}, u32[]{:S(2)}, u32[]{:S(2)}) collective-permute-start(bf16[64,512]{1,0:T(8,128)(2,1)S(1)} %collective-permute-done.7), channel_id=1, source_target_pairs={{260,256},{261,257},{262,258},{263,259},{256,260},{257,261},{258,2... | collective-permute-start | bytes 196616 | tf_op jit(solution)/shard_map/ppermute | solution.py:261
  31.9 1.2 %copy-start = (bf16[512,1024]{1,0:T(8,128)(2,1)S(1)}, bf16[512,1024]{1,0:T(8,128)(2,1)}, u32[]{:S(2)}) copy-start(bf16[512,1024]{1,0:T(8,128)(2,1)} %key_up) | copy-start | bytes 3145732
  33.1 1.2 %copy-start.1 = (bf16[512,1024]{1,0:T(8,128)(2,1)S(1)}, bf16[512,1024]{1,0:T(8,128)(2,1)}, u32[]{:S(2)}) copy-start(bf16[512,1024]{1,0:T(8,128)(2,1)} %value_up) | copy-start | bytes 3145732
  34.3 13.4 %copy-start.7 = (bf16[512,1536]{1,0:T(8,128)(2,1)S(1)}, bf16[512,1536]{1,0:T(8,128)(2,1)}, u32[]{:S(2)}) copy-start(bf16[512,1536]{1,0:T(8,128)(2,1)} %queries.3) | copy-start | bytes 4718596
  34.7 17.9 %collective-permute-start.1 = (bf16[208,512]{1,0:T(8,128)(2,1)S(1)}, bf16[208,512]{1,0:T(8,128)(2,1)S(1)}, u32[]{:S(2)}, u32[]{:S(2)}) collective-permute-start(bf16[208,512]{1,0:T(8,128)(2,1)S(1)} %pad_maximum_fusion.1), channel_id=1, source_target_pairs={{0,8},{1,9},{2,10},{3,11},{4,12},{5,13},{6,14},{7,15},{8,16},{9,17... | collective-permute-start | bytes 638984 | tf_op jit(solution)/shard_map/ppermute | solution.py:261
  36.2 16.4 %collective-permute-start.5 = (bf16[384,512]{1,0:T(8,128)(2,1)S(1)}, bf16[384,512]{1,0:T(8,128)(2,1)S(1)}, u32[]{:S(2)}, u32[]{:S(2)}) collective-permute-start(bf16[384,512]{1,0:T(8,128)(2,1)S(1)} %pad_maximum_fusion), channel_id=1, source_target_pairs={{0,8},{1,9},{2,10},{3,11},{4,12},{5,13},{6,14},{7,15},{8,16},{9,17... | collective-permute-start | bytes 1179656 | tf_op jit(solution)/shard_map/ppermute | solution.py:261
  37.6 14.1 %collective-permute-start.11 = (bf16[128,512]{1,0:T(8,128)(2,1)S(1)}, bf16[128,512]{1,0:T(8,128)(2,1)S(1)}, u32[]{:S(2)}, u32[]{:S(2)}) collective-permute-start(bf16[128,512]{1,0:T(8,128)(2,1)S(1)} %constant_dynamic-update-slice_fusion.wa), channel_id=1, source_target_pairs={{259,256},{258,257},{257,258},{256,259},{263,260},{262,261},{261,2... | collective-permute-start | bytes 393224 | tf_op jit(solution)/shard_map/ppermute | solution.py:261
  40.4 11.3 %collective-permute-start.10 = (bf16[128,512]{1,0:T(8,128)(2,1)S(1)}, bf16[128,512]{1,0:T(8,128)(2,1)S(1)}, u32[]{:S(2)}, u32[]{:S(2)}) collective-permute-start(bf16[128,512]{1,0:T(8,128)(2,1)S(1)} %constant_dynamic-update-slice_fusion.wa), channel_id=1, source_target_pairs={{258,256},{259,257},{256,258},{257,259},{262,260},{263,261},{260,2... | collective-permute-start | bytes 393224 | tf_op jit(solution)/shard_map/ppermute | solution.py:261
  45.8 6.9 %collective-permute-start.9 = (bf16[128,512]{1,0:T(8,128)(2,1)S(1)}, bf16[128,512]{1,0:T(8,128)(2,1)S(1)}, u32[]{:S(2)}, u32[]{:S(2)}) collective-permute-start(bf16[128,512]{1,0:T(8,128)(2,1)S(1)} %constant_dynamic-update-slice_fusion.wa), channel_id=1, source_target_pairs={{257,256},{256,257},{259,258},{258,259},{261,260},{260,261},{263,2... | collective-permute-start | bytes 393224 | tf_op jit(solution)/shard_map/ppermute | solution.py:261

commit v4 on v3

--- a/solution.py
+++ b/solution.py
@@ -26,6 +26,10 @@
 
 def place(pieces, at, first, lat):
     rows = [(piece, r) for piece in pieces for r in range(0, piece.shape[0], SHARD)]
+    if first is None:
+        for (piece, r), which in zip(rows, ORDER, strict=True):
+            lat[pl.ds(pl.multiple_of((at ^ which) * SHARD, SHARD), SHARD), :] = piece[r : r + SHARD, :]
+        return
     other = pl.multiple_of(BLOCK - first, BLOCK)
     for (piece, r), which in zip(rows, ORDER, strict=True):
         to = pl.ds(pl.multiple_of((at ^ which) * SHARD, SHARD), SHARD)
@@ -34,8 +38,11 @@
 
 
 def place_rope(rope_in, first, keys):
-    other = pl.multiple_of(BLOCK - first, BLOCK)
-    rope = jnp.concatenate([rope_in[:, pl.ds(first, BLOCK)], rope_in[:, pl.ds(other, BLOCK)]], axis=1)
+    if first is None:
+        rope = rope_in[...]
+    else:
+        other = pl.multiple_of(BLOCK - first, BLOCK)
+        rope = jnp.concatenate([rope_in[:, pl.ds(first, BLOCK)], rope_in[:, pl.ds(other, BLOCK)]], axis=1)
     none = jnp.zeros_like(rope)
     for head in range(keys.shape[0]):
         if head % 2 == 0:
@@ -95,7 +102,7 @@
             top_out[pl.ds(at, BLOCK), columns] = jnp.broadcast_to(top, (BLOCK, VAL))
 
 
-def prior_kernel(ids, queries, near, far, there, across, key_up_t, value_up, acc_in, sum_in, top_in, out, lat, keys, values, tail):
+def prior_kernel(ids, queries, near, far, there, across, key_up_t, value_up, acc_in, sum_in, top_in, out, lat, keys, values, tail, done, sent):
     turn = lax.axis_size("seq") // 2
     crossing = lax.rem(lax.axis_index("seq"), turn) == 0
     spot = lax.axis_index("head")
@@ -108,23 +115,28 @@
 
     pl.when(crossing)(tail_from(there.at[SHARD:]))
     pl.when(jnp.logical_not(crossing))(tail_from(near.at[NEAR * SHARD :]))
+    pl.when(crossing)(lambda: place(across, spot ^ 4, None, lat))
+    pl.when(jnp.logical_not(crossing))(lambda: place((near.at[: NEAR * SHARD], far), spot, None, lat))
+    place_rope(tail.at[:ROPE], None, keys)
+    project(lat, key_up_t, value_up, keys, values)
     one = jnp.max(tail[ROPE : ROPE + 1, :128].astype(F32)).astype(jnp.int32)
     two = jnp.max(tail[ROPE : ROPE + 1, BLOCK : BLOCK + 128].astype(F32)).astype(jnp.int32)
     first = pl.multiple_of(jnp.where(one < two, 0, BLOCK), BLOCK)
     low, high = jnp.minimum(one, two), jnp.maximum(one, two)
-    pl.when(crossing)(lambda: place(across, spot ^ 4, first, lat))
-    pl.when(jnp.logical_not(crossing))(lambda: place((near.at[: NEAR * SHARD], far), spot, first, lat))
-    place_rope(tail.at[:ROPE], first, keys)
-    project(lat, key_up_t, value_up, keys, values)
     heads = keys.shape[0]
     ones = jnp.ones((2 * BLOCK, VAL), BF16)
 
+    def leave(rows, half):
+        columns = slice(half * heads // 2 * VAL, (half + 1) * heads // 2 * VAL)
+        return pltpu.make_async_copy(done.at[rows, columns], out.at[rows, columns], sent.at[half])
+
     def merged(start, size, many):
         rows = slice(start, start + size)
+        seen = pl.ds(first if many == BLOCK else 0, many)
 
         def scores(head):
             base = (head // 2) * 384 + (head % 2) * 128
-            return dot(queries[rows, base : base + 256], keys[head, :, :many])
+            return dot(queries[rows, base : base + 256], keys[head, :, seen])
 
         def body():
             ahead = scores(0)
@@ -133,20 +145,33 @@
                 if head + 1 < heads:
                     ahead = scores(head + 1)
                 columns = slice(head * VAL, (head + 1) * VAL)
-                value = jnp.concatenate([values[:many, columns], ones[:many]], axis=1)
+                value = jnp.concatenate([values[seen, columns], ones[:many]], axis=1)
                 before = top_in[rows, columns]
                 top = jnp.maximum(before, jnp.max(score, axis=1, keepdims=True))
                 weight = jnp.exp2((score - jnp.concatenate([top] * (many // VAL), axis=1)) * GAIN).astype(BF16)
                 keep = jnp.exp2((before - top) * GAIN)
                 got = dot(weight, value)
                 total = got[:, VAL:] + sum_in[rows, columns] * keep
-                out[rows, columns] = ((got[:, :VAL] + acc_in[rows, columns] * keep) / total).astype(BF16)
+                done[rows, columns] = ((got[:, :VAL] + acc_in[rows, columns] * keep) / total).astype(BF16)
+                if head == heads // 2 - 1:
+                    leave(rows, 0).start()
+            leave(rows, 1).start()
+            leave(rows, 0).wait()
+            leave(rows, 1).wait()
 
         return body
 
     def alone(start):
         rows = slice(start, start + BLOCK)
-        return lambda: out.__setitem__((rows, slice(None)), (acc_in[rows, :] / sum_in[rows, :]).astype(BF16))
+
+        def body():
+            done[rows, :] = (acc_in[rows, :] / sum_in[rows, :]).astype(BF16)
+            for half in range(2):
+                leave(rows, half).start()
+            for half in range(2):
+                leave(rows, half).wait()
+
+        return body
 
     counts = [(low <= ids[part]).astype(jnp.int32) + (high <= ids[part]).astype(jnp.int32) for part in range(2)]
     whole = jnp.logical_and(counts[0] == 2, counts[1] == 2)
@@ -194,8 +219,12 @@
         kernel,
         out_shape=jax.ShapeDtypeStruct((tokens, heads * VAL), BF16),
         in_specs=[SMEM] + [VMEM] * 13,
-        out_specs=VMEM,
-        scratch_shapes=scratch_of(tokens, heads, value_up.shape[0]) + [pltpu.VMEM((ROPE + ID_ROWS, tokens), BF16)],
+        out_specs=pl.BlockSpec(memory_space=pl.ANY),
+        scratch_shapes=scratch_of(tokens, heads, value_up.shape[0]) + [
+            pltpu.VMEM((ROPE + ID_ROWS, tokens), BF16),
+            pltpu.VMEM((tokens, heads * VAL), BF16),
+            pltpu.SemaphoreType.DMA((2,)),
+        ],
         compiler_params=pltpu.CompilerParams(vmem_limit_bytes=20 << 20),
         cost_estimate=pl.CostEstimate(flops=4 << 30, bytes_accessed=8 << 20, transcendentals=1 << 21),
         name="prior_part",

time: 58.7 us -> 58.2 us (level)
  Pallas kernels: 10.6 us -> 9.68 us
    pallas_call x1, Pallas kernels: 5.71 us -> 4.82 us  [prior_part(): pl.pallas_call(kernel, out_shape=jax.ShapeDtypeStruct((tokens, heads * VA...]
where the time goes in v4:
time: 58.2 us; the launch traced here: 57.6 us
  starting transfers between devices  41.7 us (72%)
  Pallas kernels  9.68 us (17%)
  local copies, waits for them, and re-layouts  4.81 us (8%)
  waiting for transfers between devices  0.95 us (2%)
    ppermute x8, starting transfers between devices, onward(): return lax.ppermute(shard, both, sent)  22.6 us
    ppermute x4, starting transfers between devices, swapped(): lax.ppermute(shard, 'head', [(i, i ^ by) for i in range(lax.axis_size('he...  19.1 us
    pallas_call x1, Pallas kernels, prior_part(): pl.pallas_call(kernel, out_shape=jax.ShapeDtypeStruct((tokens, heads * VA...  4.82 us
    unnamed x17, local copies, waits for them, and re-layouts  4.79 us
    pallas_call x1, Pallas kernels, own_part(): pl.pallas_call(own_kernel, out_shape=(jax.ShapeDtypeStruct((tokens, heads...  3.95 us
  transfers between devices with their start and end apart: 12, of which 1 were waited for; matrix products, arithmetic and copies ran while one was open for 0% of the time, Pallas kernels for 8%

profile of v4, /device:TPU:64, one launch (start us, length us, event | category | flops | bytes accessed | tf_op | source)
XLA Modules:
  0.0 57.6 jit_solution(16771768425198988851)
XLA Ops:
  0.0 9.1 %collective-permute-start = (bf16[64,512]{1,0:T(8,128)(2,1)}, bf16[64,512]{1,0:T(8,128)(2,1)S(1)}, u32[]{:S(2)}, u32[]{:S(2)}) collective-permute-start(bf16[64,512]{1,0:T(8,128)(2,1)} %bitcast.2), channel_id=1, source_target_pairs={{0,4},{1,5},{2,6},{3,7},{4,0},{5,1},{6,2},{7,3},{8,12},{9,13},{10,... | collective-permute-start | bytes 196616 | tf_op jit(solution)/shard_map/ppermute | solution.py:270
  9.1 1.3 %collective-permute-start.7 = (bf16[64,512]{1,0:T(8,128)(2,1)}, bf16[64,512]{1,0:T(8,128)(2,1)S(1)}, u32[]{:S(2)}, u32[]{:S(2)}) collective-permute-start(bf16[64,512]{1,0:T(8,128)(2,1)} %bitcast.3), channel_id=1, source_target_pairs={{252,256},{253,257},{254,258},{255,259},{248,260},{249,261},{250,2... | collective-permute-start | bytes 196616 | tf_op jit(solution)/shard_map/ppermute | solution.py:290
  10.4 0.8 %copy-done.2 = bf16[512,64]{0,1:T(8,128)(2,1)S(1)} copy-done((bf16[512,64]{0,1:T(8,128)(2,1)S(1)}, bf16[512,64]{0,1:T(8,128)(2,1)}, u32[]{:S(2)}) %copy-start.2) | copy-done | bytes 65560
  11.2 0.8 %copy-done.3 = bf16[512,64]{0,1:T(8,128)(2,1)S(1)} copy-done((bf16[512,64]{0,1:T(8,128)(2,1)S(1)}, bf16[512,64]{0,1:T(8,128)(2,1)}, u32[]{:S(2)}) %copy-start.3) | copy-done | bytes 65560
  12.1 0.7 %copy-done.5 = s32[2]{0:T(128)S(1)} copy-done((s32[2]{0:T(128)S(1)}, s32[2]{0:T(128)}, u32[]{:S(2)}) %copy-start.5) | copy-done | bytes 32
  12.7 0.6 leaving_part.1
  13.3 0.0 copy-start.4
  13.3 0.0 copy-start.6
  13.3 1.4 %collective-permute-start.6 = (bf16[144,512]{1,0:T(8,128)(2,1)S(1)}, bf16[144,512]{1,0:T(8,128)(2,1)S(1)}, u32[]{:S(2)}, u32[]{:S(2)}) collective-permute-start(bf16[144,512]{1,0:T(8,128)(2,1)S(1)} %leaving_part.1), channel_id=1, source_target_pairs={{252,256},{253,257},{254,258},{255,259},{248,260},{249,261},{250,2... | collective-permute-start | bytes 442376 | tf_op jit(solution)/shard_map/ppermute | solution.py:290
  14.8 0.0 collective-permute-done
  14.8 2.0 %collective-permute-start.4 = (bf16[128,512]{1,0:T(8,128)(2,1)S(1)}, bf16[128,512]{1,0:T(8,128)(2,1)S(1)}, u32[]{:S(2)}, u32[]{:S(2)}) collective-permute-start(bf16[128,512]{1,0:T(8,128)(2,1)S(1)} %pad_maximum_fusion.2.a), channel_id=1, source_target_pairs={{0,3},{1,2},{2,1},{3,0},{4,7},{5,6},{6,5},{7,4},{8,11},{9,10},{10,... | collective-permute-start | bytes 393224 | tf_op jit(solution)/shard_map/ppermute | solution.py:270
  16.8 6.1 %collective-permute-start.3 = (bf16[128,512]{1,0:T(8,128)(2,1)S(1)}, bf16[128,512]{1,0:T(8,128)(2,1)S(1)}, u32[]{:S(2)}, u32[]{:S(2)}) collective-permute-start(bf16[128,512]{1,0:T(8,128)(2,1)S(1)} %pad_maximum_fusion.2.a), channel_id=1, source_target_pairs={{0,2},{1,3},{2,0},{3,1},{4,6},{5,7},{6,4},{7,5},{8,10},{9,11},{10,... | collective-permute-start | bytes 393224 | tf_op jit(solution)/shard_map/ppermute | solution.py:270
  22.9 1.9 %collective-permute-start.2 = (bf16[128,512]{1,0:T(8,128)(2,1)S(1)}, bf16[128,512]{1,0:T(8,128)(2,1)S(1)}, u32[]{:S(2)}, u32[]{:S(2)}) collective-permute-start(bf16[128,512]{1,0:T(8,128)(2,1)S(1)} %pad_maximum_fusion.2.a), channel_id=1, source_target_pairs={{0,1},{1,0},{2,3},{3,2},{4,5},{5,4},{6,7},{7,6},{8,9},{9,8},{10,11... | collective-permute-start | bytes 393224 | tf_op jit(solution)/shard_map/ppermute | solution.py:270
  24.8 0.0 collective-permute-done.7
  24.9 7.0 %collective-permute-start.8 = (bf16[64,512]{1,0:T(8,128)(2,1)S(1)}, bf16[64,512]{1,0:T(8,128)(2,1)S(1)}, u32[]{:S(2)}, u32[]{:S(2)}) collective-permute-start(bf16[64,512]{1,0:T(8,128)(2,1)S(1)} %collective-permute-done.7), channel_id=1, source_target_pairs={{260,256},{261,257},{262,258},{263,259},{256,260},{257,261},{258,2... | collective-permute-start | bytes 196616 | tf_op jit(solution)/shard_map/ppermute | solution.py:290
  31.9 0.0 copy-start
  31.9 1.2 %copy-done = bf16[512,1024]{1,0:T(8,128)(2,1)S(1)} copy-done((bf16[512,1024]{1,0:T(8,128)(2,1)S(1)}, bf16[512,1024]{1,0:T(8,128)(2,1)}, u32[]{:S(2)}) %copy-start) | copy-done | bytes 1048600
  33.1 1.2 %copy-done.1 = bf16[512,1024]{1,0:T(8,128)(2,1)S(1)} copy-done((bf16[512,1024]{1,0:T(8,128)(2,1)S(1)}, bf16[512,1024]{1,0:T(8,128)(2,1)}, u32[]{:S(2)}) %copy-start.1) | copy-done | bytes 1048600
  34.3 0.4 weights_part.1
  34.7 0.0 collective-permute-done.4.d
  34.7 1.4 %collective-permute-start.1 = (bf16[208,512]{1,0:T(8,128)(2,1)S(1)}, bf16[208,512]{1,0:T(8,128)(2,1)S(1)}, u32[]{:S(2)}, u32[]{:S(2)}) collective-permute-start(bf16[208,512]{1,0:T(8,128)(2,1)S(1)} %pad_maximum_fusion.1), channel_id=1, source_target_pairs={{0,8},{1,9},{2,10},{3,11},{4,12},{5,13},{6,14},{7,15},{8,16},{9,17... | collective-permute-start | bytes 638984 | tf_op jit(solution)/shard_map/ppermute | solution.py:290
  36.2 0.0 collective-permute-done.3.c
  36.2 1.3 %collective-permute-start.5 = (bf16[384,512]{1,0:T(8,128)(2,1)S(1)}, bf16[384,512]{1,0:T(8,128)(2,1)S(1)}, u32[]{:S(2)}, u32[]{:S(2)}) collective-permute-start(bf16[384,512]{1,0:T(8,128)(2,1)S(1)} %pad_maximum_fusion), channel_id=1, source_target_pairs={{0,8},{1,9},{2,10},{3,11},{4,12},{5,13},{6,14},{7,15},{8,16},{9,17... | collective-permute-start | bytes 1179656 | tf_op jit(solution)/shard_map/ppermute | solution.py:290
  37.6 2.8 %collective-permute-start.11 = (bf16[128,512]{1,0:T(8,128)(2,1)S(1)}, bf16[128,512]{1,0:T(8,128)(2,1)S(1)}, u32[]{:S(2)}, u32[]{:S(2)}) collective-permute-start(bf16[128,512]{1,0:T(8,128)(2,1)S(1)} %constant_dynamic-update-slice_fusion.wa), channel_id=1, source_target_pairs={{259,256},{258,257},{257,258},{256,259},{263,260},{262,261},{261,2... | collective-permute-start | bytes 393224 | tf_op jit(solution)/shard_map/ppermute | solution.py:290
  40.4 5.4 %collective-permute-start.10 = (bf16[128,512]{1,0:T(8,128)(2,1)S(1)}, bf16[128,512]{1,0:T(8,128)(2,1)S(1)}, u32[]{:S(2)}, u32[]{:S(2)}) collective-permute-start(bf16[128,512]{1,0:T(8,128)(2,1)S(1)} %constant_dynamic-update-slice_fusion.wa), channel_id=1, source_target_pairs={{258,256},{259,257},{256,258},{257,259},{262,260},{263,261},{260,2... | collective-permute-start | bytes 393224 | tf_op jit(solution)/shard_map/ppermute | solution.py:290
  45.8 0.0 collective-permute-done.6.there
  45.8 1.9 %collective-permute-start.9 = (bf16[128,512]{1,0:T(8,128)(2,1)S(1)}, bf16[128,512]{1,0:T(8,128)(2,1)S(1)}, u32[]{:S(2)}, u32[]{:S(2)}) collective-permute-start(bf16[128,512]{1,0:T(8,128)(2,1)S(1)} %constant_dynamic-update-slice_fusion.wa), channel_id=1, source_target_pairs={{257,256},{256,257},{259,258},{258,259},{261,260},{260,261},{263,2... | collective-permute-start | bytes 393224 | tf_op jit(solution)/shard_map/ppermute | solution.py:290
  47.7 4.0 %own_part.1 = (f32[512,1024]{1,0:T(8,128)S(1)}, f32[512,1024]{1,0:T(8,128)S(1)}, f32[512,1024]{1,0:T(8,128)S(1)}) custom-call(s32[2]{0:T(128)S(1)} %copy-done.6, bf16[512,1536]{1,0:T(8,128)(2,1)S(1)} %copy-done.7, bf16[128,512]{1,0:T(8,128)(2,1)S(1)} %pad_maximum_fusion.2.a, bf16[128,512]{1,0:T(8,128)(2,1)S(1)} %collective-permute-done.2.b, ...), custom_call_target="tpu_custom_call" | custom-call | flops 3221225472 | bytes 8388608 | tf_op jit(solution)/shard_map/own_part/pallas_call | solution.py:200
  51.7 0.0 collective-permute-done.11.wd
  51.7 0.9 %collective-permute-done.9.wb = bf16[128,512]{1,0:T(8,128)(2,1)S(1)} collective-permute-done((bf16[128,512]{1,0:T(8,128)(2,1)S(1)}, bf16[128,512]{1,0:T(8,128)(2,1)S(1)}, u32[]{:S(2)}, u32[]{:S(2)}) %collective-permute-start.9) | collective-permute-done | bytes 131104 | tf_op jit(solution)/shard_map/ppermute | solution.py:290
  52.6 0.0 collective-permute-done.1.near
  52.6 4.8 %prior_part.1 = bf16[512,1024]{1,0:T(8,128)(2,1)} custom-call(s32[2]{0:T(128)S(1)} %copy-done.6, bf16[512,1536]{1,0:T(8,128)(2,1)S(1)} %copy-done.7, bf16[208,512]{1,0:T(8,128)(2,1)S(1)} %collective-permute-done.1.near, bf16[384,512]{1,0:T(8,128)(2,1)S(1)} %collective-permute-done.5.far, bf16[144,512]{1,0:T(8,128)(2,1)S(1)} %collective-permute-done.6.there, ...), custom_call_target="tpu_custom_call" | custom-call | flops 4294967296 | bytes 8388608 | tf_op jit(solution)/shard_map/prior_part/pallas_call | solution.py:218
  (19 shorter events, 0.1 us)
Async XLA Ops:
  0.0 14.8 %collective-permute-start = (bf16[64,512]{1,0:T(8,128)(2,1)}, bf16[64,512]{1,0:T(8,128)(2,1)S(1)}, u32[]{:S(2)}, u32[]{:S(2)}) collective-permute-start(bf16[64,512]{1,0:T(8,128)(2,1)} %bitcast.2), channel_id=1, source_target_pairs={{0,4},{1,5},{2,6},{3,7},{4,0},{5,1},{6,2},{7,3},{8,12},{9,13},{10,... | collective-permute-start | bytes 196616 | tf_op jit(solution)/shard_map/ppermute | solution.py:270
  9.1 15.8 %collective-permute-start.7 = (bf16[64,512]{1,0:T(8,128)(2,1)}, bf16[64,512]{1,0:T(8,128)(2,1)S(1)}, u32[]{:S(2)}, u32[]{:S(2)}) collective-permute-start(bf16[64,512]{1,0:T(8,128)(2,1)} %bitcast.3), channel_id=1, source_target_pairs={{252,256},{253,257},{254,258},{255,259},{248,260},{249,261},{250,2... | collective-permute-start | bytes 196616 | tf_op jit(solution)/shard_map/ppermute | solution.py:290
  10.4 0.8 %copy-start.2 = (bf16[512,64]{0,1:T(8,128)(2,1)S(1)}, bf16[512,64]{0,1:T(8,128)(2,1)}, u32[]{:S(2)}) copy-start(bf16[512,64]{0,1:T(8,128)(2,1)} %param.7) | copy-start | bytes 196612
  11.2 0.8 %copy-start.3 = (bf16[512,64]{0,1:T(8,128)(2,1)S(1)}, bf16[512,64]{0,1:T(8,128)(2,1)}, u32[]{:S(2)}) copy-start(bf16[512,64]{0,1:T(8,128)(2,1)} %param.8) | copy-start | bytes 196612
  12.1 0.7 %copy-start.5 = (s32[2]{0:T(128)S(1)}, s32[2]{0:T(128)}, u32[]{:S(2)}) copy-start(s32[2]{0:T(128)} %ids.5) | copy-start | bytes 28
  13.3 34.4 %copy-start.4 = (bf16[512,64]{0,1:T(8,128)(2,1)S(1)}, bf16[512,64]{0,1:T(8,128)(2,1)}, u32[]{:S(2)}) copy-start(bf16[512,64]{0,1:T(8,128)(2,1)} %param.8) | copy-start | bytes 196612
  13.3 34.4 %copy-start.6 = (s32[2]{0:T(128)S(1)}, s32[2]{0:T(128)}, u32[]{:S(2)}) copy-start(s32[2]{0:T(128)} %ids.5) | copy-start | bytes 28
  13.3 32.5 %collective-permute-start.6 = (bf16[144,512]{1,0:T(8,128)(2,1)S(1)}, bf16[144,512]{1,0:T(8,128)(2,1)S(1)}, u32[]{:S(2)}, u32[]{:S(2)}) collective-permute-start(bf16[144,512]{1,0:T(8,128)(2,1)S(1)} %leaving_part.1), channel_id=1, source_target_pairs={{252,256},{253,257},{254,258},{255,259},{248,260},{249,261},{250,2... | collective-permute-start | bytes 442376 | tf_op jit(solution)/shard_map/ppermute | solution.py:290
  14.8 19.9 %collective-permute-start.4 = (bf16[128,512]{1,0:T(8,128)(2,1)S(1)}, bf16[128,512]{1,0:T(8,128)(2,1)S(1)}, u32[]{:S(2)}, u32[]{:S(2)}) collective-permute-start(bf16[128,512]{1,0:T(8,128)(2,1)S(1)} %pad_maximum_fusion.2.a), channel_id=1, source_target_pairs={{0,3},{1,2},{2,1},{3,0},{4,7},{5,6},{6,5},{7,4},{8,11},{9,10},{10,... | collective-permute-start | bytes 393224 | tf_op jit(solution)/shard_map/ppermute | solution.py:270
  16.8 19.3 %collective-permute-start.3 = (bf16[128,512]{1,0:T(8,128)(2,1)S(1)}, bf16[128,512]{1,0:T(8,128)(2,1)S(1)}, u32[]{:S(2)}, u32[]{:S(2)}) collective-permute-start(bf16[128,512]{1,0:T(8,128)(2,1)S(1)} %pad_maximum_fusion.2.a), channel_id=1, source_target_pairs={{0,2},{1,3},{2,0},{3,1},{4,6},{5,7},{6,4},{7,5},{8,10},{9,11},{10,... | collective-permute-start | bytes 393224 | tf_op jit(solution)/shard_map/ppermute | solution.py:270
  22.9 13.3 %collective-permute-start.2 = (bf16[128,512]{1,0:T(8,128)(2,1)S(1)}, bf16[128,512]{1,0:T(8,128)(2,1)S(1)}, u32[]{:S(2)}, u32[]{:S(2)}) collective-permute-start(bf16[128,512]{1,0:T(8,128)(2,1)S(1)} %pad_maximum_fusion.2.a), channel_id=1, source_target_pairs={{0,1},{1,0},{2,3},{3,2},{4,5},{5,4},{6,7},{7,6},{8,9},{9,8},{10,11... | collective-permute-start | bytes 393224 | tf_op jit(solution)/shard_map/ppermute | solution.py:270
  24.9 12.7 %collective-permute-start.8 = (bf16[64,512]{1,0:T(8,128)(2,1)S(1)}, bf16[64,512]{1,0:T(8,128)(2,1)S(1)}, u32[]{:S(2)}, u32[]{:S(2)}) collective-permute-start(bf16[64,512]{1,0:T(8,128)(2,1)S(1)} %collective-permute-done.7), channel_id=1, source_target_pairs={{260,256},{261,257},{262,258},{263,259},{256,260},{257,261},{258,2... | collective-permute-start | bytes 196616 | tf_op jit(solution)/shard_map/ppermute | solution.py:290
  31.9 1.2 %copy-start = (bf16[512,1024]{1,0:T(8,128)(2,1)S(1)}, bf16[512,1024]{1,0:T(8,128)(2,1)}, u32[]{:S(2)}) copy-start(bf16[512,1024]{1,0:T(8,128)(2,1)} %key_up) | copy-start | bytes 3145732
  33.1 1.2 %copy-start.1 = (bf16[512,1024]{1,0:T(8,128)(2,1)S(1)}, bf16[512,1024]{1,0:T(8,128)(2,1)}, u32[]{:S(2)}) copy-start(bf16[512,1024]{1,0:T(8,128)(2,1)} %value_up) | copy-start | bytes 3145732
  34.3 13.4 %copy-start.7 = (bf16[512,1536]{1,0:T(8,128)(2,1)S(1)}, bf16[512,1536]{1,0:T(8,128)(2,1)}, u32[]{:S(2)}) copy-start(bf16[512,1536]{1,0:T(8,128)(2,1)} %queries.3) | copy-start | bytes 4718596
  34.7 17.9 %collective-permute-start.1 = (bf16[208,512]{1,0:T(8,128)(2,1)S(1)}, bf16[208,512]{1,0:T(8,128)(2,1)S(1)}, u32[]{:S(2)}, u32[]{:S(2)}) collective-permute-start(bf16[208,512]{1,0:T(8,128)(2,1)S(1)} %pad_maximum_fusion.1), channel_id=1, source_target_pairs={{0,8},{1,9},{2,10},{3,11},{4,12},{5,13},{6,14},{7,15},{8,16},{9,17... | collective-permute-start | bytes 638984 | tf_op jit(solution)/shard_map/ppermute | solution.py:290
  36.2 16.4 %collective-permute-start.5 = (bf16[384,512]{1,0:T(8,128)(2,1)S(1)}, bf16[384,512]{1,0:T(8,128)(2,1)S(1)}, u32[]{:S(2)}, u32[]{:S(2)}) collective-permute-start(bf16[384,512]{1,0:T(8,128)(2,1)S(1)} %pad_maximum_fusion), channel_id=1, source_target_pairs={{0,8},{1,9},{2,10},{3,11},{4,12},{5,13},{6,14},{7,15},{8,16},{9,17... | collective-permute-start | bytes 1179656 | tf_op jit(solution)/shard_map/ppermute | solution.py:290
  37.6 14.1 %collective-permute-start.11 = (bf16[128,512]{1,0:T(8,128)(2,1)S(1)}, bf16[128,512]{1,0:T(8,128)(2,1)S(1)}, u32[]{:S(2)}, u32[]{:S(2)}) collective-permute-start(bf16[128,512]{1,0:T(8,128)(2,1)S(1)} %constant_dynamic-update-slice_fusion.wa), channel_id=1, source_target_pairs={{259,256},{258,257},{257,258},{256,259},{263,260},{262,261},{261,2... | collective-permute-start | bytes 393224 | tf_op jit(solution)/shard_map/ppermute | solution.py:290
  40.4 11.3 %collective-permute-start.10 = (bf16[128,512]{1,0:T(8,128)(2,1)S(1)}, bf16[128,512]{1,0:T(8,128)(2,1)S(1)}, u32[]{:S(2)}, u32[]{:S(2)}) collective-permute-start(bf16[128,512]{1,0:T(8,128)(2,1)S(1)} %constant_dynamic-update-slice_fusion.wa), channel_id=1, source_target_pairs={{258,256},{259,257},{256,258},{257,259},{262,260},{263,261},{260,2... | collective-permute-start | bytes 393224 | tf_op jit(solution)/shard_map/ppermute | solution.py:290
  45.8 6.9 %collective-permute-start.9 = (bf16[128,512]{1,0:T(8,128)(2,1)S(1)}, bf16[128,512]{1,0:T(8,128)(2,1)S(1)}, u32[]{:S(2)}, u32[]{:S(2)}) collective-permute-start(bf16[128,512]{1,0:T(8,128)(2,1)S(1)} %constant_dynamic-update-slice_fusion.wa), channel_id=1, source_target_pairs={{257,256},{256,257},{259,258},{258,259},{261,260},{260,261},{263,2... | collective-permute-start | bytes 393224 | tf_op jit(solution)/shard_map/ppermute | solution.py:290
